TPU v7x, 512 devices: a whole 4x4x16 slice. The times are simulated.
512 devices in a mesh: dp: 64 (over z, y), mp: 8 (over x, core).
Axes of the slice: x: 4, y: 4, z: 16, core: 2. Of those that a mesh axis runs over, the one named last changes fastest.
Arguments:
- tokens: bfloat16 [1024, 144, 512], P(('dp', 'mp')), may hold values from -6 to 6
- cotangent: bfloat16 [1024, 144, 512], P(('dp', 'mp')), may hold values from -6 to 6
- region_ids: int32 [1024, 144], P(('dp', 'mp')), may hold values from 0 to 3
- rel_bucket: int32 [144, 144], replicated, may hold values from 0 to 758
- norm_gain: float32 [512], replicated, may hold values from 0.5 to 1.5
- in_weight: bfloat16 [512, 1536], P('mp'), may hold values from -0.25 to 0.25
- out_weight: bfloat16 [512, 512], P('mp'), may hold values from -0.25 to 0.25
- bias_table: float32 [8, 759], replicated, may hold values from -3 to 250
- in_error: float32 [64, 512, 1536], P('dp', 'mp'), may hold values from -12 to 12
- out_error: float32 [64, 512, 512], P('dp', 'mp'), may hold values from -6 to 6
- in_basis: float32 [8, 1536, 32], P('mp'), may hold values from -6 to 6
- out_basis: float32 [8, 512, 32], P('mp'), may hold values from -6 to 6
Outputs:
- token_grad: bfloat16 [1024, 144, 512], P(('dp', 'mp'))
- gain_grad: float32 [512], replicated
- table_grad: float32 [8, 759], replicated
- in_update: float32 [512, 1536], P('mp')
- out_update: float32 [512, 512], P('mp')
- in_new_error: float32 [64, 512, 1536], P('dp', 'mp')
- out_new_error: float32 [64, 512, 512], P('dp', 'mp')
- in_new_basis: float32 [8, 1536, 32], P('mp')
- out_new_basis: float32 [8, 512, 32], P('mp')
All inputs are finite; a program needn't handle non-finite values.
Results may differ from a plain program's by a relative error of at most 0.024.
Values may be sent and summed in bfloat16 or wider, within the bound.
A program may use at most 64 MiB of HBM per device.

v0:
```python
import jax
import jax.numpy as jnp
from jax import lax
from jax.sharding import PartitionSpec as P

NORM_EPS = 1e-05
BASIS_EPS = 1e-06
MASKED = -1e30
HIGH = lax.Precision.HIGHEST


def norm_forward(token_rows):
    tokens_wide = token_rows.astype(jnp.float32)
    mean_x = jnp.mean(tokens_wide, axis=-1, keepdims=True)
    centered = tokens_wide - mean_x
    variance = jnp.mean(centered * centered, axis=-1, keepdims=True)
    inv_sigma = lax.rsqrt(variance + NORM_EPS)
    return (centered * inv_sigma, inv_sigma)


def orthonormal(left_factor):

    def next_column(j, finished):
        j = j.astype(jnp.int32)
        column = lax.dynamic_slice_in_dim(left_factor, j, 1, 1)
        for repeat in range(2):
            column = column - jnp.dot(
                finished, jnp.dot(finished.T, column, precision=HIGH), precision=HIGH
            )
        column = column * lax.rsqrt(jnp.sum(column * column) + BASIS_EPS)
        return lax.dynamic_update_slice_in_dim(finished, column, j, 1)

    return lax.fori_loop(0, left_factor.shape[1], next_column, jnp.zeros_like(left_factor))


def left_term(merged, basis):
    return jnp.dot(merged, basis, precision=HIGH)


def right_term(merged, left_basis):
    return jnp.einsum("rc,rk->ck", merged, left_basis, precision=HIGH)


def attention_forward(tokens, region_ids, rel_bucket, norm_gain, full_in, bias_table):
    window_count, win_span, feature_count = tokens.shape
    head_count = bias_table.shape[0]
    head_size = feature_count // head_count
    row_count = window_count * win_span
    score_scale = head_size ** (-0.5)
    x_hat, inv_sigma = norm_forward(tokens.reshape(row_count, feature_count))
    normed = (x_hat * norm_gain).astype(jnp.bfloat16)
    projected = jnp.dot(normed, full_in, preferred_element_type=jnp.float32).astype(jnp.bfloat16)
    projected = projected.reshape(window_count, win_span, 3, head_count, head_size)
    queries = projected[:, :, 0]
    key_rows = projected[:, :, 1]
    value_rows = projected[:, :, 2]
    pos_bias = jnp.take(bias_table, rel_bucket, axis=1)
    allowed = region_ids[:, :, None] == region_ids[:, None, :]
    scores = (
        jnp.einsum("wihd,wjhd->whij", queries, key_rows, preferred_element_type=jnp.float32)
        * score_scale
        + pos_bias[None]
    )
    scores = jnp.where(allowed[:, None], scores, MASKED)
    row_top = jnp.max(scores, axis=-1, keepdims=True)
    exp_scores = jnp.exp(scores - row_top)
    attn_prob = exp_scores / jnp.sum(exp_scores, axis=-1, keepdims=True)
    prob_b = attn_prob.astype(jnp.bfloat16)
    mixed_out = jnp.einsum(
        "whij,wjhd->wihd", prob_b, value_rows, preferred_element_type=jnp.float32
    )
    mixed_out = mixed_out.astype(jnp.bfloat16).reshape(row_count, feature_count)
    return (x_hat, inv_sigma, normed, queries, key_rows, value_rows, attn_prob, prob_b, mixed_out)


def attention_backward(saved, cot_rows, rel_bucket, norm_gain, full_in, full_out, table_size):
    x_hat, inv_sigma, normed, queries, key_rows, value_rows, attn_prob, prob_b, mixed_out = saved
    window_count, win_span, head_count, head_size = queries.shape
    row_count = window_count * win_span
    feature_count = head_count * head_size
    score_scale = head_size ** (-0.5)
    mixed_grad = jnp.einsum("te,de->td", cot_rows, full_out, preferred_element_type=jnp.float32)
    mixed_grad = mixed_grad.astype(jnp.bfloat16).reshape(
        window_count, win_span, head_count, head_size
    )
    prob_grad = jnp.einsum(
        "wihd,wjhd->whij", mixed_grad, value_rows, preferred_element_type=jnp.float32
    )
    value_grad = jnp.einsum(
        "whij,wihd->wjhd", prob_b, mixed_grad, preferred_element_type=jnp.float32
    )
    score_grad = attn_prob * (prob_grad - jnp.sum(attn_prob * prob_grad, axis=-1, keepdims=True))
    score_sum = jnp.sum(score_grad, axis=0).reshape(head_count, win_span * win_span)
    table_term = jax.ops.segment_sum(score_sum.T, rel_bucket.reshape(-1), num_segments=table_size).T
    score_b = score_grad.astype(jnp.bfloat16)
    query_grad = (
        jnp.einsum("whij,wjhd->wihd", score_b, key_rows, preferred_element_type=jnp.float32)
        * score_scale
    )
    key_grad = (
        jnp.einsum("whij,wihd->wjhd", score_b, queries, preferred_element_type=jnp.float32)
        * score_scale
    )
    packed_grad = jnp.stack([query_grad, key_grad, value_grad], axis=2).astype(jnp.bfloat16)
    packed_grad = packed_grad.reshape(row_count, 3 * feature_count)
    normed_grad = jnp.einsum("tc,dc->td", packed_grad, full_in, preferred_element_type=jnp.float32)
    gain_term = jnp.sum(normed_grad * x_hat, axis=0)
    hat_grad = normed_grad * norm_gain
    token_delta = inv_sigma * (
        hat_grad
        - jnp.mean(hat_grad, axis=-1, keepdims=True)
        - x_hat * jnp.mean(hat_grad * x_hat, axis=-1, keepdims=True)
    )
    token_grad = (cot_rows.astype(jnp.float32) + token_delta).astype(jnp.bfloat16)
    in_term = jnp.einsum("td,tc->dc", normed, packed_grad, preferred_element_type=jnp.float32)
    return (token_grad, in_term, gain_term, table_term)


def shards(
    tokens,
    cotangent,
    region_ids,
    rel_bucket,
    norm_gain,
    in_weight,
    out_weight,
    bias_table,
    in_error,
    out_error,
    in_basis,
    out_basis,
):
    n_dp = lax.axis_size("dp")
    n_mp = lax.axis_size("mp")
    full_in, full_out = (
        lax.all_gather(in_weight, "mp", axis=0, tiled=True),
        lax.all_gather(out_weight, "mp", axis=0, tiled=True),
    )
    saved = attention_forward(tokens, region_ids, rel_bucket, norm_gain, full_in, bias_table)
    row_count = tokens.shape[0] * tokens.shape[1]
    cot_rows = cotangent.reshape(row_count, tokens.shape[2])
    mixed_out = saved[8]
    out_term = jnp.einsum("td,te->de", mixed_out, cot_rows, preferred_element_type=jnp.float32)
    table_size = bias_table.shape[1]
    token_grad, in_term, gain_term, table_term = attention_backward(
        saved, cot_rows, rel_bucket, norm_gain, full_in, full_out, table_size
    )
    in_shard, out_shard = (
        lax.psum_scatter(
            in_term.astype(jnp.bfloat16), "mp", scatter_dimension=0, tiled=True
        ).astype(jnp.float32),
        lax.psum_scatter(
            out_term.astype(jnp.bfloat16), "mp", scatter_dimension=0, tiled=True
        ).astype(jnp.float32),
    )
    in_merged = in_shard / n_mp + in_error[0]
    out_merged = out_shard / n_mp + out_error[0]
    in_left, out_left = lax.psum(
        (left_term(in_merged, in_basis[0]), left_term(out_merged, out_basis[0])), "dp"
    )
    in_ortho = orthonormal(in_left / n_dp)
    out_ortho = orthonormal(out_left / n_dp)
    in_right, out_right = lax.psum(
        (right_term(in_merged, in_ortho), right_term(out_merged, out_ortho)), "dp"
    )
    in_right = in_right / n_dp
    out_right = out_right / n_dp
    in_update = jnp.dot(in_ortho, in_right.T, precision=HIGH)
    out_update = jnp.dot(out_ortho, out_right.T, precision=HIGH)
    in_new_error = in_merged - in_update
    out_new_error = out_merged - out_update
    gain_total, table_total = lax.psum((gain_term, table_term), ("dp", "mp"))
    devices = n_dp * n_mp
    return (
        token_grad.reshape(tokens.shape),
        gain_total / devices,
        table_total / devices,
        in_update,
        out_update,
        in_new_error[None],
        out_new_error[None],
        in_right[None],
        out_right[None],
    )


def solution(mesh):
    placed = (
        P(("dp", "mp"), None, None),
        P(("dp", "mp"), None, None),
        P(("dp", "mp"), None),
        P(),
        P(),
        P("mp", None),
        P("mp", None),
        P(),
        P("dp", "mp", None),
        P("dp", "mp", None),
        P("mp", None, None),
        P("mp", None, None),
    )
    return jax.shard_map(
        shards,
        mesh=mesh,
        in_specs=placed,
        out_specs=(
            P(("dp", "mp"), None, None),
            P(),
            P(),
            P("mp", None),
            P("mp", None),
            P("dp", "mp", None),
            P("dp", "mp", None),
            P("mp", None, None),
            P("mp", None, None),
        ),
        check_vma=False,
    )
```

profile of v0, /device:TPU:1, one launch (start us, length us, event | category | flops | bytes accessed | tf_op | source)
XLA Modules:
  0.0 1015.2 jit_solution(9241922168968255913)
XLA Ops:
  8.0 1.1 convert_reduce_fusion
  9.2 1.2 multiply_reduce_fusion.5
  10.5 20.2 %all_gather.7 = bf16[512,512]{1,0:T(8,128)(2,1)S(1)} all-gather(bf16[64,512]{1,0:T(8,128)(2,1)} %param.22), channel_id=1, replica_groups=mesh['dp'=64,'mp'=8] {'mp'}, dimensions={0}, use_global_device_ids=true | all-gather | bytes 589824 | tf_op jit(solution)/shard_map/all_gather | solution.py:137
  30.7 1.3 convolution_convert_fusion.4
  32.3 1.2 copy.70
  33.9 38.9 %gather_fusion = f32[20736,8]{1,0:T(8,128)} fusion(f32[8,759]{0,1:T(8,128)S(1)} %copy.67, s32[21504]{0:T(1024)S(1)} %pad_clamp_fusion), kind=kCustom, calls=%fused_computation | custom fusion | bytes 1410048 | tf_op jit(solution)/shard_map/jit(_take)/gather | solution.py:57
  72.8 11.3 %copy.68 = f32[144,144,8]{0,1,2:T(8,128)S(1)} copy(f32[144,144,8]{2,1,0:T(8,128)} %bitcast.201) | data formatting | bytes 1327104 | tf_op jit(solution)/shard_map/jit(_take)/gather | solution.py:57
  84.4 0.9 multiply_convert_fusion
  85.4 1.2 select_bitcast_fusion
  86.6 2.0 convolution_convert_fusion.1
  88.7 1.1 reshape.164
  89.7 1.1 fusion.61
  90.9 2.2 copy.85
  93.1 1.2 copy.86
  94.3 1.2 copy.87
  95.5 2.7 fusion.62
  98.2 2.6 fusion.8
  100.9 2.0 multiply_reduce_fusion.2
  102.8 1.4 copy.79
  104.6 1.3 convolution_convert_fusion.2
  106.2 3.1 fusion.13
  111.7 1.5 maximum_convert_fusion
  113.2 2.9 copy.75
  116.2 1.9 convert_element_type.79
  118.0 3.5 convolution_convert_fusion
  122.9 6.1 copy.77
  129.1 112.5 %scatter_custom_fusion = f32[759,8]{1,0:T(8,128)S(1)} fusion(s32[20736]{0:T(1024)S(1)} %reshape.180, f32[20736,8]{1,0:T(8,128)} %copy.77, f32[]{:T(128)} %constant.109.clone.1), kind=kCustom, calls=%fused_computation.73 | custom fusion | flops 165888 | bytes 24800 | tf_op jit(solution)/shard_map/scatter-add | solution.py:94
  241.6 2.5 multiply_reduce_fusion.6
  244.1 107.5 %all-reduce = (f32[512]{0:T(512)S(1)}, f32[8,759]{0,1:T(8,128)S(1)}) all-reduce(f32[512]{0:T(512)S(1)} %get-tuple-element.177, f32[8,759]{0,1:T(8,128)S(1)} %bitcast.203), channel_id=1, replica_groups=mesh['dp'=64,'mp'=8] {'dp','mp'}, use_global_device_ids=true, to_apply=%region_8.9 | all-reduce | flops 6584 | bytes 52672 | tf_op jit(solution)/shard_map/psum | solution.py:172
  351.7 1.1 fusion.43
  352.9 1.4 fusion.27
  354.3 222.7 %all-reduce.1 = (f32[64,32]{0,1:T(8,128)S(1)}, f32[64,32]{0,1:T(8,128)S(1)}) all-reduce(f32[64,32]{0,1:T(8,128)S(1)} %fusion.27, f32[64,32]{0,1:T(8,128)S(1)} %fusion.43), channel_id=1, replica_groups=mesh['dp'=64,'mp'=8] {'dp'}, use_global_device_ids=true, to_apply=%region_13.14 | all-reduce | flops 4096 | bytes 32768 | tf_op jit(solution)/shard_map/psum | solution.py:158
  577.0 61.8 %while.26 = (s32[]{:T(128)}, f32[64,32]{0,1:T(8,128)S(1)}, f32[64,32]{0,1:T(8,128)S(1)}, s32[]{:T(128)}, f32[]{:T(128)}, /*index=5*/s32[]{:T(128)}) while((s32[]{:T(128)}, f32[64,32]{0,1:T(8,128)S(1)}, f32[64,32]{0,1:T(8,128)S(1)}, s32[]{:T(128)}, f32[]{:T(128)}, /*index=5*/s32[]{:T(128)}) %tuple.75), condition=%wide.region_16.17_spmd, body=%wide.region_14.16_spmd.sunk | while | flops 98626 | bytes 44405 | solution.py:33
  577.5 0.8 multiply_reduce_fusion.9
  579.4 0.8 multiply_reduce_fusion.9
  581.3 0.8 multiply_reduce_fusion.9
  583.3 0.8 multiply_reduce_fusion.9
  585.2 0.8 multiply_reduce_fusion.9
  587.1 0.8 multiply_reduce_fusion.9
  589.1 0.8 multiply_reduce_fusion.9
  591.0 0.8 multiply_reduce_fusion.9
  592.9 0.8 multiply_reduce_fusion.9
  594.8 0.8 multiply_reduce_fusion.9
  604.5 0.8 multiply_reduce_fusion.9
  606.4 0.8 multiply_reduce_fusion.9
  608.4 0.8 multiply_reduce_fusion.9
  610.3 0.8 multiply_reduce_fusion.9
  612.2 0.8 multiply_reduce_fusion.9
  638.9 61.8 %while.27 = (s32[]{:T(128)}, f32[64,32]{0,1:T(8,128)S(1)}, f32[64,32]{0,1:T(8,128)S(1)}, s32[]{:T(128)}, f32[]{:T(128)}, /*index=5*/s32[]{:T(128)}) while((s32[]{:T(128)}, f32[64,32]{0,1:T(8,128)S(1)}, f32[64,32]{0,1:T(8,128)S(1)}, s32[]{:T(128)}, f32[]{:T(128)}, /*index=5*/s32[]{:T(128)}) %tuple.78), condition=%wide.region_22.23_spmd, body=%wide.region_20.22_spmd.sunk | while | flops 98626 | bytes 44405 | solution.py:33
  639.3 0.8 multiply_reduce_fusion.10
  668.3 0.8 multiply_reduce_fusion.10
  670.2 0.8 multiply_reduce_fusion.10
  672.1 0.8 multiply_reduce_fusion.10
  674.1 0.8 multiply_reduce_fusion.10
  676.0 0.8 multiply_reduce_fusion.10
  700.7 1.1 fusion.41
  701.8 0.9 fusion.47
  704.0 1.0 add_convert_fusion
  705.0 296.3 %all-reduce.5.cloned.1.call-done = (f32[1536,32]{0,1:T(8,128)}, f32[512,32]{0,1:T(8,128)}) async-done(((f32[1536,32]{0,1:T(8,128)}, f32[512,32]{0,1:T(8,128)}), (f32[1536,32]{0,1:T(8,128)}, f32[512,32]{0,1:T(8,128)})) %all-reduce.5.cloned.1.call-update) | async-done | bytes 262160 | tf_op jit(solution)/shard_map/psum | solution.py:163
  1001.2 1.4 fusion.31
  1002.7 1.8 multiply_bitcast_fusion
  1004.5 1.1 fusion.45
  1005.6 1.5 multiply_bitcast_fusion.1
  1007.2 0.8 subtract_bitcast_fusion
  (450 shorter events, 70.3 us)
Async XLA Ops:
  7.2 345.7 %copy-start = (f32[1,1536,32]{1,2,0:T(8,128)S(1)}, f32[1,1536,32]{1,2,0:T(8,128)}, u32[]{:S(2)}) copy-start(f32[1,1536,32]{1,2,0:T(8,128)} %param.26) | copy-start | bytes 589828
  7.2 79.4 %all-gather.2.cloned.1.call-start = ((), (), s32[]{:S(2)}) async-start(), calls=%async_computation.2 | async-start | bytes 1769472 | tf_op jit(solution)/shard_map/all_gather | solution.py:136
  7.9 343.7 %reduce-scatter.5.cloned.1.call-start = ((), (), s32[]{:S(2)}) async-start(), calls=%async_computation.4 | async-start | bytes 589824 | tf_op jit(solution)/shard_map/reduce_scatter | solution.py:152
  10.5 23.1 %copy-start.21 = (f32[8,759]{1,0:T(8,128)S(1)}, f32[8,759]{1,0:T(8,128)}, u32[]{:S(2)}) copy-start(f32[8,759]{1,0:T(8,128)} %param.23) | copy-start | bytes 72868
  30.7 3.1 copy-start.9
  72.8 11.5 %copy-start.23 = (s32[2,144]{1,0:T(2,128)S(1)}, s32[2,144]{1,0:T(2,128)}, u32[]{:S(2)}) copy-start(s32[2,144]{1,0:T(2,128)} %param.18) | copy-start | bytes 3460
  72.8 11.6 %copy-start.1 = (bf16[2,144,512]{2,1,0:T(8,128)(2,1)S(1)}, bf16[2,144,512]{2,1,0:T(8,128)(2,1)}, u32[]{:S(2)}) copy-start(bf16[2,144,512]{2,1,0:T(8,128)(2,1)} %param.16) | copy-start | bytes 884740
  72.8 11.6 %copy-start.22 = (f32[512]{0:T(512)S(1)}, f32[512]{0:T(512)}, u32[]{:S(2)}) copy-start(f32[512]{0:T(512)} %param.20) | copy-start | bytes 6148
  85.4 1.2 copy-start.16
  98.2 2.7 copy-start.3
  98.2 2.7 copy-start.18
  98.2 2.7 copy-start.19
  102.8 1.8 copy-start.12
  106.0 246.9 %reduce-scatter.3.cloned.1.call-start = ((), (), s32[]{:S(2)}) async-start(), calls=%async_computation.3 | async-start | bytes 1769472 | tf_op jit(solution)/shard_map/reduce_scatter | solution.py:149
  106.2 3.2 copy-start.6
  109.3 1.0 copy-start.5
  109.4 1.8 copy-start.4
  118.0 3.6 copy-start.10
  121.6 879.7 %all-reduce.5.cloned.1.call-start = ((), (), s32[]{:S(2)}) async-start(), calls=%async_computation.5 | async-start | bytes 524288 | tf_op jit(solution)/shard_map/psum | solution.py:163
  122.9 118.7 %copy-start.14 = (bf16[288,1536]{1,0:T(8,128)(2,1)S(1)}, bf16[288,1536]{1,0:T(8,128)(2,1)}, u32[]{:S(2)}) copy-start(bf16[288,1536]{1,0:T(8,128)(2,1)} %convert_element_type.79) | copy-start | bytes 2654212
  241.6 110.1 %copy-start.11 = (f32[1,64,512]{2,1,0:T(8,128)S(1)}, f32[1,64,512]{2,1,0:T(8,128)}, u32[]{:S(2)}) copy-start(f32[1,64,512]{2,1,0:T(8,128)} %param.25) | copy-start | bytes 393220
  241.6 110.0 %copy-start.20 = (f32[1,512,32]{1,2,0:T(8,128)S(1)}, f32[1,512,32]{1,2,0:T(8,128)}, u32[]{:S(2)}) copy-start(f32[1,512,32]{1,2,0:T(8,128)} %param.27) | copy-start | bytes 196612
  241.6 111.3 %copy-start.2 = (f32[1,64,1536]{2,1,0:T(8,128)S(1)}, f32[1,64,1536]{2,1,0:T(8,128)}, u32[]{:S(2)}) copy-start(f32[1,64,1536]{2,1,0:T(8,128)} %param.24) | copy-start | bytes 1179652
  351.7 350.1 %copy-start.15 = (bf16[64,512]{1,0:T(8,128)(2,1)S(1)}, bf16[64,512]{1,0:T(8,128)(2,1)}, u32[]{:S(2)}) copy-start(bf16[64,512]{1,0:T(8,128)(2,1)} %reduce-scatter.5.cloned.1.call-done) | copy-start | bytes 196612
  352.8 351.2 %copy-start.13 = (bf16[2,144,512]{2,1,0:T(8,128)(2,1)S(1)}, bf16[2,144,512]{2,1,0:T(8,128)(2,1)}, u32[]{:S(2)}) copy-start(bf16[2,144,512]{2,1,0:T(8,128)(2,1)} %param.17) | copy-start | bytes 884740
  352.9 347.8 %copy-start.7 = (bf16[64,1536]{1,0:T(8,128)(2,1)S(1)}, bf16[64,1536]{1,0:T(8,128)(2,1)}, u32[]{:S(2)}) copy-start(bf16[64,1536]{1,0:T(8,128)(2,1)} %reduce-scatter.3.cloned.1.call-done) | copy-start | bytes 589828
  1002.7 6.0 copy-start.8
  1005.6 3.0 copy-start.17
Sparse Core Ops, SparseCore 0:
  10.1 37.6 all-gather.1
  106.1 35.3 reduce-scatter.4
  144.6 39.0 reduce-scatter.2
  702.8 298.4 all-reduce.4
where the time goes:
time: 1030 us; the launch traced here: 1020 us
  blocking collectives  350 us (34%)
  waiting for transfers between devices  297 us (29%)
  other arithmetic  129 us (13%)
  matrix products  102 us (10%)
  local copies, waits for them, and re-layouts  77.3 us (8%)
  loops' own time  45.7 us (4%)
  between operations  14.3 us (1%)
    psum x1, waiting for transfers between devices, shards(): lax.psum((right_term(in_merged, in_ortho), right_term(out_merged, out_ort...  296 us
    psum x1, blocking collectives, shards(): lax.psum((left_term(in_merged, in_basis[0]), left_term(out_merged, out_ba...  223 us
    scatter-add x1, other arithmetic, attention_backward(): jax.ops.segment_sum(score_sum.T, rel_bucket.reshape(-1), num_segments=tab...  113 us
    psum x1, blocking collectives, shards(): gain_total, table_total = lax.psum((gain_term, table_term), ('dp', 'mp'))  107 us
    dot_general x128, matrix products, next_column(): jnp.dot(finished, jnp.dot(finished.T, column, precision=HIGH), precision=...  57.9 us
    gather x2, local copies, waits for them, and re-layouts, attention_forward(): pos_bias = jnp.take(bias_table, rel_bucket, axis=1)  50.1 us
    another operation x2, loops' own time, orthonormal(): lax.fori_loop(0, left_factor.shape[1], next_column, jnp.zeros_like(left_f...  45.7 us
  transfers between devices with their start and end apart: 4, of which 1 were waited for; matrix products, arithmetic and copies ran while one was open for 20% of the time, Pallas kernels for 0%

commit v1 on v0

v1 whole, which is shorter than its diff:
```python
import functools

import jax
import jax.numpy as jnp
from jax import lax
from jax.experimental import pallas as pl
from jax.experimental.pallas import tpu as pltpu
from jax.sharding import PartitionSpec as P

NORM_EPS = 1e-05
BASIS_EPS = 1e-06
MASKED = -1e30
HIGH = lax.Precision.HIGHEST
MESH = pl.DeviceIdType.MESH
F32 = jnp.float32
BF16 = jnp.bfloat16
VMEM = pl.BlockSpec(memory_space=pltpu.VMEM)

WIN, SPAN, WIDTH, HEADS, CHUNKS = 2, 144, 512, 8, 6
ROWS = WIN * SPAN
N_X, N_Y, N_Z, N_MP = 4, 4, 16, 8
BLOCK = 64
COLS = 4 * WIDTH


def nt(a, b, **kw):
    return lax.dot_general(a, b, (((1,), (1,)), ((), ())), preferred_element_type=F32, **kw)


def tn(a, b, **kw):
    return lax.dot_general(a, b, (((0,), (0,)), ((), ())), preferred_element_type=F32, **kw)


def nn(a, b, **kw):
    return jnp.dot(a, b, preferred_element_type=F32, **kw)


def gather_kernel(in_ref, out_ref, full_in, full_out, send, recv, fsend, frecv, local):
    mp = lax.axis_index("mp")
    x, core = mp // 2, mp % 2
    sibling = {"mp": 2 * x + 1 - core}

    def peer(step):
        return {"mp": 2 * ((x + step) % N_X) + core}

    barrier = pltpu.get_barrier_semaphore()
    for target in (sibling, peer(1), peer(2), peer(3)):
        pl.semaphore_signal(barrier, inc=1, device_id=target, device_id_type=MESH)

    def rows(index):
        return pl.ds(pl.multiple_of(index * BLOCK, BLOCK), BLOCK)

    arrays = ((in_ref, full_in), (out_ref, full_out))
    own = [pltpu.make_async_copy(src, full.at[rows(mp)], local.at[k]) for k, (src, full) in enumerate(arrays)]
    for copy in own:
        copy.start()
    pl.semaphore_wait(barrier, 4)

    first = {}
    for step in (2, 1, 3):
        for k, (src, full) in enumerate(arrays):
            first[step, k] = pltpu.make_async_remote_copy(
                src, full.at[rows(mp)], send.at[k, step - 1], recv.at[k, step - 1], device_id=peer(step), device_id_type=MESH
            )
            first[step, k].start()
    forward = []
    for k, (src, full) in enumerate(arrays):
        copy = pltpu.make_async_remote_copy(
            src, full.at[rows(mp)], fsend.at[k, 0], frecv.at[k, 0], device_id=sibling, device_id_type=MESH
        )
        copy.start()
        forward.append(copy)
    for k in range(2):
        for step in (1, 3, 2):
            full = arrays[k][1]
            first[step, k].wait_recv()
            slab = full.at[rows(2 * ((x + N_X - step) % N_X) + core)]
            copy = pltpu.make_async_remote_copy(
                slab, slab, fsend.at[k, step], frecv.at[k, step], device_id=sibling, device_id_type=MESH
            )
            copy.start()
            forward.append(copy)
    for copy in own:
        copy.wait()
    for copy in first.values():
        copy.wait_send()
    for copy in forward:
        copy.wait()


def gather_weights(in_weight, out_weight):
    return pl.pallas_call(
        gather_kernel,
        out_shape=(
            jax.ShapeDtypeStruct((WIDTH, 3 * WIDTH), BF16),
            jax.ShapeDtypeStruct((WIDTH, WIDTH), BF16),
        ),
        in_specs=[VMEM, VMEM],
        out_specs=(VMEM, VMEM),
        scratch_shapes=[
            pltpu.SemaphoreType.DMA((2, 3)),
            pltpu.SemaphoreType.DMA((2, 3)),
            pltpu.SemaphoreType.DMA((2, 4)),
            pltpu.SemaphoreType.DMA((2, 4)),
            pltpu.SemaphoreType.DMA((2,)),
        ],
        compiler_params=pltpu.CompilerParams(collective_id=0, has_side_effects=True, vmem_limit_bytes=32 << 20),
        name="gather_weights",
    )(in_weight, out_weight)


def bias_kernel(table_ref, bucket_ref, bias_ref, wide):
    wide[...] = jnp.zeros_like(wide)
    wide[:, :SPAN] = bucket_ref[...]
    for part in range(2):
        lanes = 128 if part == 0 else SPAN - 128
        start = part * 128

        @pl.loop(0, SPAN // 16)
        def _(block):
            at = pl.ds(pl.multiple_of(block * 16, 16), 16)
            index = wide[at, pl.ds(start, 128)]
            low = index & 127
            chunk = index >> 7
            for head in range(HEADS):
                found = jnp.zeros((16, 128), F32)
                for c in range(CHUNKS):
                    row = jnp.broadcast_to(table_ref[head : head + 1, c * 128 : (c + 1) * 128], (16, 128))
                    found = jnp.where(chunk == c, jnp.take_along_axis(row, low, axis=1), found)
                bias_ref[head, at, start : start + lanes] = found[:, :lanes]


def bias_lookup(table, bucket):
    return pl.pallas_call(
        bias_kernel,
        out_shape=jax.ShapeDtypeStruct((HEADS, SPAN, SPAN), F32),
        in_specs=[VMEM, VMEM],
        out_specs=VMEM,
        scratch_shapes=[pltpu.VMEM((SPAN, 256), jnp.int32)],
        compiler_params=pltpu.CompilerParams(vmem_limit_bytes=32 << 20),
        name="bias_lookup",
    )(table, bucket)


def attention_kernel(
    tok_ref, cot_ref, region_ref, bucket_ref, bias_ref, gain_ref, win_ref, wout_ref,
    tokgrad_ref, term_ref, extra_ref,
    proj, mixgrad, mixed, packed, score_sum,
):
    gain = gain_ref[...]
    wide = tok_ref[...].astype(F32)
    centered = wide - jnp.mean(wide, axis=-1, keepdims=True)
    inv_sigma = lax.rsqrt(jnp.mean(centered * centered, axis=-1, keepdims=True) + NORM_EPS)
    x_hat = centered * inv_sigma
    normed = (x_hat * gain).astype(BF16)
    proj[...] = nn(normed, win_ref[...]).astype(BF16)
    mixgrad[...] = nt(cot_ref[...], wout_ref[...]).astype(BF16)

    lane = lax.broadcasted_iota(jnp.int32, (1, 128), 1)
    first_half = lane < 64
    halves = (first_half.astype(BF16), (lane >= 64).astype(BF16))
    scale = jnp.asarray(0.125, BF16)
    for w in range(WIN):
        region = region_ref[w : w + 1, :].astype(F32)
        square = jnp.broadcast_to(region, (SPAN, SPAN))
        allowed = square == square.T
        rows = slice(w * SPAN, (w + 1) * SPAN)
        for pair in range(HEADS // 2):
            at = [slice(k * WIDTH + pair * 128, k * WIDTH + (pair + 1) * 128) for k in range(3)]
            q = proj[rows, at[0]] * scale
            key = proj[rows, at[1]]
            value = proj[rows, at[2]]
            key_scaled = key * scale
            grad = mixgrad[rows, at[0]]
            parts = []
            for t in range(2):
                head = 2 * pair + t
                scores = nt(q * halves[t], key) + bias_ref[head]
                scores = jnp.where(allowed, scores, MASKED)
                exps = jnp.exp(scores - jnp.max(scores, axis=-1, keepdims=True))
                prob = exps * (1.0 / jnp.sum(exps, axis=-1, keepdims=True))
                prob_b = prob.astype(BF16)
                out = nn(prob_b, value)
                prob_grad = nt(grad * halves[t], value)
                value_grad = tn(prob_b, grad)
                score_grad = prob * (prob_grad - jnp.sum(prob * prob_grad, axis=-1, keepdims=True))
                if w == 0:
                    score_sum[head] = score_grad
                else:
                    score_sum[head] += score_grad
                score_b = score_grad.astype(BF16)
                parts.append((nn(score_b, key_scaled), tn(score_b, q), value_grad, out))
            merged = [jnp.where(first_half, a, b).astype(BF16) for a, b in zip(*parts)]
            for k in range(3):
                packed[rows, at[k]] = merged[k]
            mixed[rows, at[0]] = merged[3]

    term_ref[:, : 3 * WIDTH] = tn(normed, packed[...]).astype(BF16)
    term_ref[:, 3 * WIDTH :] = tn(mixed[...], cot_ref[...]).astype(BF16)

    normed_grad = nt(packed[...], win_ref[...])
    gain_term = jnp.sum(normed_grad * x_hat, axis=0, keepdims=True)
    hat_grad = normed_grad * gain
    delta = inv_sigma * (
        hat_grad
        - jnp.mean(hat_grad, axis=-1, keepdims=True)
        - x_hat * jnp.mean(hat_grad * x_hat, axis=-1, keepdims=True)
    )
    tokgrad_ref[...] = (cot_ref[...].astype(F32) + delta).astype(BF16)

    chunk_row = lax.broadcasted_iota(jnp.int32, (8, SPAN), 0)
    within = lax.broadcasted_iota(jnp.int32, (128, SPAN), 0)

    def add_row(i, total):
        bucket = bucket_ref[pl.ds(i, 1), :]
        chunk_is = jnp.broadcast_to(bucket >> 7, (8, SPAN)) == chunk_row
        one_hot = jnp.where(jnp.broadcast_to(bucket & 127, (128, SPAN)) == within, 1.0, 0.0).astype(BF16)
        picked = jnp.concatenate(
            [
                jnp.where(chunk_is, jnp.broadcast_to(score_sum[head, pl.ds(i, 1), :], (8, SPAN)), 0.0)
                for head in range(HEADS)
            ],
            axis=0,
        )
        high = picked.astype(BF16)
        low = (picked - high.astype(F32)).astype(BF16)
        return total + nt(jnp.concatenate([high, low], axis=0), one_hot)

    total = lax.fori_loop(0, SPAN, add_row, jnp.zeros((128, 128), F32))
    table_term = total[:64] + total[64:]
    for head in range(HEADS):
        extra_ref[head] = table_term[8 * head : 8 * head + 8]
        part = gain_term[:, 128 * (head // 2) : 128 * (head // 2 + 1)]
        if head % 2:
            part = pltpu.roll(part, 64, 1)
        extra_ref[head, 6:7, :] = part


def attention(tok, cot, region, bucket, bias, gain, full_in, full_out):
    return pl.pallas_call(
        attention_kernel,
        out_shape=(
            jax.ShapeDtypeStruct((ROWS, WIDTH), BF16),
            jax.ShapeDtypeStruct((WIDTH, COLS), BF16),
            jax.ShapeDtypeStruct((HEADS, 8, 128), F32),
        ),
        in_specs=[VMEM] * 8,
        out_specs=(VMEM, VMEM, VMEM),
        scratch_shapes=[
            pltpu.VMEM((ROWS, 3 * WIDTH), BF16),
            pltpu.VMEM((ROWS, WIDTH), BF16),
            pltpu.VMEM((ROWS, WIDTH), BF16),
            pltpu.VMEM((ROWS, 3 * WIDTH), BF16),
            pltpu.VMEM((HEADS, SPAN, SPAN), F32),
        ],
        compiler_params=pltpu.CompilerParams(vmem_limit_bytes=48 << 20),
        name="attention",
    )(tok, cot, region, bucket, bias, gain, full_in, full_out)


def scatter_kernel(
    term, extra, in_error, out_error, merged, extra_sum,
    near, near_x, mine, far, far_x, mine_x,
    s_near, r_near, s_near_x, r_near_x, s_far, r_far, s_far_x, r_far_x,
):
    mp = lax.axis_index("mp")
    x, core = mp // 2, mp % 2
    sibling = {"mp": 2 * x + 1 - core}

    def chip(step):
        return (x + step) % N_X

    def peer(step):
        return {"mp": 2 * chip(step) + core}

    barrier = pltpu.get_barrier_semaphore()
    for target in (sibling, peer(1), peer(2), peer(3)):
        pl.semaphore_signal(barrier, inc=1, device_id=target, device_id_type=MESH)
    pl.semaphore_wait(barrier, 4)

    order = (2, 1, 3, 0)
    first = {}
    for step in order:
        first[step] = (
            pltpu.make_async_remote_copy(
                term.at[chip(step), 1 - core], near.at[step], s_near.at[step], r_near.at[step],
                device_id=sibling, device_id_type=MESH,
            ),
            pltpu.make_async_remote_copy(
                extra.at[chip(step), 1 - core], near_x.at[step], s_near_x.at[step], r_near_x.at[step],
                device_id=sibling, device_id_type=MESH,
            ),
        )
        for copy in first[step]:
            copy.start()
    second = {}
    for step in order[:3]:
        for copy in first[step]:
            copy.wait_recv()
        mine[step] = (term[chip(step), core].astype(F32) + near[step].astype(F32)).astype(BF16)
        mine_x[step] = extra[chip(step), core] + near_x[step]
        second[step] = (
            pltpu.make_async_remote_copy(
                mine.at[step], far.at[step], s_far.at[step], r_far.at[step],
                device_id=peer(step), device_id_type=MESH,
            ),
            pltpu.make_async_remote_copy(
                mine_x.at[step], far_x.at[step], s_far_x.at[step], r_far_x.at[step],
                device_id=peer(step), device_id_type=MESH,
            ),
        )
        for copy in second[step]:
            copy.start()
    for copy in first[0]:
        copy.wait_recv()
    total = term[x, core].astype(F32) + near[0].astype(F32)
    total_x = extra[x, core] + near_x[0]
    for step in (1, 3, 2):
        for copy in second[step]:
            copy.wait_recv()
        total = total + far[step].astype(F32)
        total_x = total_x + far_x[step]
    total = total * (1.0 / N_MP)
    merged[:, : 3 * WIDTH] = total[:, : 3 * WIDTH] + in_error[...]
    merged[:, 3 * WIDTH :] = total[:, 3 * WIDTH :] + out_error[...]
    extra_sum[...] = total_x
    for step in order:
        for copy in first[step]:
            copy.wait_send()
    for step in order[:3]:
        for copy in second[step]:
            copy.wait_send()


def scatter_terms(term, extra, in_error, out_error):
    dma = pltpu.SemaphoreType.DMA((4,))
    return pl.pallas_call(
        scatter_kernel,
        out_shape=(jax.ShapeDtypeStruct((BLOCK, COLS), F32), jax.ShapeDtypeStruct((8, 128), F32)),
        in_specs=[VMEM] * 4,
        out_specs=(VMEM, VMEM),
        scratch_shapes=[
            pltpu.VMEM((4, BLOCK, COLS), BF16),
            pltpu.VMEM((4, 8, 128), F32),
            pltpu.VMEM((4, BLOCK, COLS), BF16),
            pltpu.VMEM((4, BLOCK, COLS), BF16),
            pltpu.VMEM((4, 8, 128), F32),
            pltpu.VMEM((4, 8, 128), F32),
        ]
        + [dma] * 8,
        compiler_params=pltpu.CompilerParams(collective_id=1, has_side_effects=True, vmem_limit_bytes=32 << 20),
        name="scatter_terms",
    )(term.reshape(N_X, 2, BLOCK, COLS), extra.reshape(N_X, 2, 8, 128), in_error, out_error)


def mean_kernel(
    merged, extra, mean, extra_all,
    y_in, z_in, slab, piece, extra_y, ex_y_in, ex_z_in, ex_part, ex_out,
    s_y, r_y, s_z, r_z, s_zz, r_zz, s_yy, r_yy,
    s_xy, r_xy, s_xz, r_xz, s_xyy, r_xyy, s_xm, r_xm,
):
    dp = lax.axis_index("dp")
    mp = lax.axis_index("mp")
    z, y = dp // N_Y, dp % N_Y

    def y_peer(step):
        return {"dp": z * N_Y + (y + step) % N_Y}

    def z_peer(step):
        return {"dp": ((z + step) % N_Z) * N_Y + y}

    def mp_peer(step):
        return {"mp": (mp + step) % N_MP}

    def remote(src, dst, send, recv, target):
        copy = pltpu.make_async_remote_copy(src, dst, send, recv, device_id=target, device_id_type=MESH)
        copy.start()
        return copy

    barrier = pltpu.get_barrier_semaphore()
    peers = [y_peer(s) for s in range(1, N_Y)] + [z_peer(s) for s in range(1, N_Z)] + [mp_peer(s) for s in range(1, N_MP)]
    for target in peers:
        pl.semaphore_signal(barrier, inc=1, device_id=target, device_id_type=MESH)
    for k in range(N_Y):
        extra_y[k] = extra[2 * k : 2 * k + 2, :]
    pl.semaphore_wait(barrier, len(peers))

    def slab_rows(index):
        return pl.ds(pl.multiple_of(index * 16, 16), 16)

    def piece_cols(index):
        return pl.ds(pl.multiple_of(index * 128, 128), 128)

    y_steps = (2, 1, 3)
    sends = []
    y_copies, ex_y = {}, {}
    for step in y_steps:
        other = (y + step) % N_Y
        ex_y[step] = remote(extra_y.at[other], ex_y_in.at[step], s_xy.at[step], r_xy.at[step], y_peer(step))
        y_copies[step] = remote(merged.at[slab_rows(other)], y_in.at[step], s_y.at[step], r_y.at[step], y_peer(step))
    part = extra_y[y]
    for step in y_steps:
        ex_y[step].wait_recv()
        part = part + ex_y_in[step]
    ex_part[...] = part
    z_steps = (8, 7, 9, 6, 10, 5, 11, 4, 12, 3, 13, 2, 14, 1, 15)
    ex_z = {s: remote(ex_part, ex_z_in.at[s], s_xz.at[s], r_xz.at[s], z_peer(s)) for s in z_steps}
    total = merged[slab_rows(y), :]
    for step in (1, 3, 2):
        y_copies[step].wait_recv()
        total = total + y_in[step]
    for k in range(N_Z):
        slab[k] = total[:, 128 * k : 128 * (k + 1)]

    z_copies = {s: remote(slab.at[(z + s) % N_Z], z_in.at[s], s_z.at[s], r_z.at[s], z_peer(s)) for s in z_steps}
    for step in reversed(z_steps):
        ex_z[step].wait_recv()
        part = part + ex_z_in[step]
    ex_out[y] = part
    ex_yy = {s: remote(ex_out.at[y], ex_out.at[y], s_xyy.at[s], r_xyy.at[s], y_peer(s)) for s in y_steps}
    own = slab[z]
    for step in reversed(z_steps):
        z_copies[step].wait_recv()
        own = own + z_in[step]
    piece[...] = own * (1.0 / (N_Y * N_Z))

    here = mean.at[slab_rows(y), piece_cols(z)]
    zz = {s: remote(piece, here, s_zz.at[s], r_zz.at[s], z_peer(s)) for s in z_steps}
    mean[slab_rows(y), piece_cols(z)] = piece[...]
    for step in y_steps:
        ex_yy[step].wait()
    for k in range(N_Y):
        extra_all[mp, 2 * k : 2 * k + 2, :] = ex_out[k]
    xm = {
        s: remote(extra_all.at[mp], extra_all.at[mp], s_xm.at[s], r_xm.at[s], mp_peer(s)) for s in range(1, N_MP)
    }
    for step in reversed(z_steps):
        zz[step].wait_recv()
    mine = mean.at[slab_rows(y)]
    yy = {s: remote(mine, mine, s_yy.at[s], r_yy.at[s], y_peer(s)) for s in y_steps}
    for copies in (y_copies, ex_y, z_copies, ex_z, zz):
        for copy in copies.values():
            copy.wait_send()
    for copies in (xm, yy):
        for copy in copies.values():
            copy.wait()


def mean_over_workers(merged, extra):
    def dma(n):
        return [pltpu.SemaphoreType.DMA((n,))] * 2

    return pl.pallas_call(
        mean_kernel,
        out_shape=(jax.ShapeDtypeStruct((BLOCK, COLS), F32), jax.ShapeDtypeStruct((N_MP, 8, 128), F32)),
        in_specs=[VMEM] * 2,
        out_specs=(VMEM, VMEM),
        scratch_shapes=[
            pltpu.VMEM((N_Y, 16, COLS), F32),
            pltpu.VMEM((N_Z, 16, 128), F32),
            pltpu.VMEM((N_Z, 16, 128), F32),
            pltpu.VMEM((16, 128), F32),
            pltpu.VMEM((N_Y, 2, 128), F32),
            pltpu.VMEM((N_Y, 2, 128), F32),
            pltpu.VMEM((N_Z, 2, 128), F32),
            pltpu.VMEM((2, 128), F32),
            pltpu.VMEM((N_Y, 2, 128), F32),
        ]
        + dma(N_Y) + dma(N_Z) + dma(N_Z) + dma(N_Y)
        + dma(N_Y) + dma(N_Z) + dma(N_Y) + dma(N_MP),
        compiler_params=pltpu.CompilerParams(collective_id=2, has_side_effects=True, vmem_limit_bytes=32 << 20),
        name="mean_over_workers",
    )(merged, extra)


def factor_kernel(
    mean, merged, in_basis, out_basis, in_update, out_update, in_error, out_error, in_right, out_right, left
):
    split = 3 * WIDTH
    left[:, :BLOCK] = nt(in_basis[...], mean[:, :split], precision=HIGH)
    left[:, BLOCK:] = nt(out_basis[...], mean[:, split:], precision=HIGH)

    lane = lax.broadcasted_iota(jnp.int32, (8, 128), 1)
    row = lax.broadcasted_iota(jnp.int32, (8, 128), 0)
    is_in = lane < BLOCK

    def half_sums(a):
        in_sum = jnp.sum(jnp.where(is_in, a, 0.0), axis=1, keepdims=True)
        out_sum = jnp.sum(jnp.where(is_in, 0.0, a), axis=1, keepdims=True)
        return jnp.where(is_in, in_sum, out_sum)

    finished = []
    for c in range(32):
        column = jnp.broadcast_to(left[c : c + 1, :], (8, 128))
        if c:
            for _ in range(2):
                taken = None
                for group in finished:
                    term = group * half_sums(group * column)
                    taken = term if taken is None else taken + term
                column = column - jnp.sum(taken, axis=0, keepdims=True)
        column = column * lax.rsqrt(half_sums(column * column) + BASIS_EPS)
        if c % 8 == 0:
            finished.append(jnp.where(row == 0, column, 0.0))
        else:
            finished[-1] = jnp.where(row == c % 8, column, finished[-1])
    ortho = jnp.concatenate(finished, axis=0)
    in_ortho, out_ortho = ortho[:, :BLOCK], ortho[:, BLOCK:]
    right = nn(in_ortho, mean[:, :split], precision=HIGH)
    in_right[...] = right
    update = tn(in_ortho, right, precision=HIGH)
    in_update[...] = update
    in_error[...] = merged[:, :split] - update
    right = nn(out_ortho, mean[:, split:], precision=HIGH)
    out_right[...] = right
    update = tn(out_ortho, right, precision=HIGH)
    out_update[...] = update
    out_error[...] = merged[:, split:] - update


def factors(mean, merged, in_basis, out_basis):
    wide = jax.ShapeDtypeStruct((BLOCK, 3 * WIDTH), F32)
    thin = jax.ShapeDtypeStruct((BLOCK, WIDTH), F32)
    return pl.pallas_call(
        factor_kernel,
        out_shape=(
            wide, thin, wide, thin,
            jax.ShapeDtypeStruct((32, 3 * WIDTH), F32),
            jax.ShapeDtypeStruct((32, WIDTH), F32),
        ),
        in_specs=[VMEM] * 4,
        out_specs=(VMEM,) * 6,
        scratch_shapes=[pltpu.VMEM((32, 128), F32)],
        compiler_params=pltpu.CompilerParams(vmem_limit_bytes=32 << 20),
        name="factors",
    )(mean, merged, in_basis, out_basis)


def shards(
    tokens,
    cotangent,
    region_ids,
    rel_bucket,
    norm_gain,
    in_weight,
    out_weight,
    bias_table,
    in_error,
    out_error,
    in_basis,
    out_basis,
):
    devices = lax.axis_size("dp") * lax.axis_size("mp")
    buckets = bias_table.shape[1]
    full_in, full_out = gather_weights(in_weight, out_weight)
    table = jnp.pad(bias_table, ((0, 0), (0, CHUNKS * 128 - buckets)))
    bias = bias_lookup(table, rel_bucket)
    token_grad, term, extra = attention(
        tokens.reshape(ROWS, WIDTH), cotangent.reshape(ROWS, WIDTH), region_ids, rel_bucket, bias,
        norm_gain.reshape(1, WIDTH), full_in, full_out,
    )
    merged, extra_sum = scatter_terms(term, extra, in_error[0], out_error[0])
    mean, extra_all = mean_over_workers(merged, extra_sum)
    in_update, out_update, in_new, out_new, in_right, out_right = factors(
        mean, merged, in_basis[0].T, out_basis[0].T
    )
    extra_all = extra_all * (1.0 / devices)
    gain_grad = extra_all[:, 6, :64].reshape(WIDTH)
    table_grad = extra_all[:, :CHUNKS, :].reshape(HEADS, CHUNKS * 128)[:, :buckets]
    return (
        token_grad.reshape(tokens.shape),
        gain_grad,
        table_grad,
        in_update,
        out_update,
        in_new[None],
        out_new[None],
        in_right.T[None],
        out_right.T[None],
    )


def solution(mesh):
    placed = (
        P(("dp", "mp"), None, None),
        P(("dp", "mp"), None, None),
        P(("dp", "mp"), None),
        P(),
        P(),
        P("mp", None),
        P("mp", None),
        P(),
        P("dp", "mp", None),
        P("dp", "mp", None),
        P("mp", None, None),
        P("mp", None, None),
    )
    return jax.shard_map(
        shards,
        mesh=mesh,
        in_specs=placed,
        out_specs=(
            P(("dp", "mp"), None, None),
            P(),
            P(),
            P("mp", None),
            P("mp", None),
            P("dp", "mp", None),
            P("dp", "mp", None),
            P("mp", None, None),
            P("mp", None, None),
        ),
        check_vma=False,
    )
```

time: 1030 us -> 140 us (0.14)
  the two profiles are of different devices: /device:TPU:1 before, /device:TPU:8 now
where the time goes in v1:
time: 140 us; the launch traced here: 139 us
  Pallas kernels  134 us (96%)
  local copies, waits for them, and re-layouts  4.75 us (3%)
    pallas_call x1, Pallas kernels, mean_over_workers(): pl.pallas_call(mean_kernel, out_shape=(jax.ShapeDtypeStruct((BLOCK, COLS)...  46.6 us
    pallas_call x1, Pallas kernels, attention(): pl.pallas_call(attention_kernel, out_shape=(jax.ShapeDtypeStruct((ROWS, W...  36.2 us
    pallas_call x1, Pallas kernels, scatter_terms(): pl.pallas_call(scatter_kernel, out_shape=(jax.ShapeDtypeStruct((BLOCK, CO...  18.8 us
    pallas_call x1, Pallas kernels, gather_weights(): pl.pallas_call(gather_kernel, out_shape=(jax.ShapeDtypeStruct((WIDTH, 3 *...  17.9 us
    pallas_call x1, Pallas kernels, factors(): pl.pallas_call(factor_kernel, out_shape=(wide, thin, wide, thin, jax.Shap...  10.9 us
    pallas_call x1, Pallas kernels, bias_lookup(): pl.pallas_call(bias_kernel, out_shape=jax.ShapeDtypeStruct((HEADS, SPAN,...  3.43 us
    unnamed x26, local copies, waits for them, and re-layouts  3.33 us

profile of v1, /device:TPU:8, one launch (start us, length us, event | category | flops | bytes accessed | tf_op | source)
XLA Modules:
  0.0 139.3 jit_solution(497904983657433239)
XLA Ops:
  0.6 0.0 copy-start.11
  0.7 0.0 copy-start.10
  0.7 0.8 pad.4.table_ref
  1.4 0.0 copy-start
  1.4 0.9 copy-done
  2.3 0.0 copy-start.1
  2.3 0.0 copy-start.3
  2.3 0.0 copy-start.4
  2.3 3.4 %bias_lookup.1.bias_ref = f32[8,144,144]{2,1,0:T(8,128)S(1)} custom-call(f32[8,768]{1,0:T(8,128)S(1)} %pad.4.table_ref, s32[144,144]{1,0:T(8,128)S(1)} %copy-done), custom_call_target="tpu_custom_call" | custom-call | tf_op jit(solution)/shard_map/bias_lookup/pallas_call | solution.py:134
  5.8 0.0 copy-start.6
  5.8 0.9 copy-done.6
  6.7 0.0 copy-start.9
  6.7 0.8 copy-done.9
  7.5 17.9 %gather_weights.1 = (bf16[512,1536]{1,0:T(8,128)(2,1)S(1)}, bf16[512,512]{1,0:T(8,128)(2,1)S(1)}) custom-call(bf16[64,1536]{1,0:T(8,128)(2,1)S(1)} %copy-done.6, bf16[64,512]{1,0:T(8,128)(2,1)S(1)} %copy-done.9), custom_call_target="tpu_custom_call" | custom-call | tf_op jit(solution)/shard_map/gather_weights/pallas_call | solution.py:92
  25.4 0.0 copy-done.11
  25.4 0.0 copy-done.10
  25.4 0.0 copy-done.1
  25.4 0.0 copy-done.3
  25.5 0.0 copy-done.4
  25.5 0.0 copy-start.2
  25.5 0.0 copy-start.7
  25.5 36.2 %attention.1 = (bf16[288,512]{1,0:T(8,128)(2,1)}, bf16[512,2048]{1,0:T(8,128)(2,1)S(1)}, f32[8,8,128]{2,1,0:T(8,128)S(1)}) custom-call(bf16[288,512]{1,0:T(8,128)(2,1)S(1)} %bitcast.30, bf16[288,512]{1,0:T(8,128)(2,1)S(1)} %bitcast.31, s32[2,144]{1,0:T(2,128)S(1)} %copy-done.10, s32[144,144]{1,0:T(8,128)S(1)} %copy-done.1, ...), custom_call_target="tpu_custom_call" | custom-call | tf_op jit(solution)/shard_map/attention/pallas_call | solution.py:240
  61.7 0.0 copy-done.2
  61.7 0.0 copy-done.7
  61.7 0.0 copy-start.5
  61.7 0.0 copy-start.8
  61.7 18.8 %scatter_terms.1 = (f32[64,2048]{1,0:T(8,128)S(1)}, f32[8,128]{1,0:T(8,128)S(1)}) custom-call(bf16[4,2,64,2048]{3,2,1,0:T(8,128)(2,1)S(1)} %bitcast.28, f32[4,2,8,128]{3,2,1,0:T(8,128)S(1)} %bitcast.35, f32[64,1536]{1,0:T(8,128)S(1)} %bitcast.29, f32[64,512]{1,0:T(8,128)S(1)} %bitcast.33), custom_call_target="tpu_custom_call" | custom-call | tf_op jit(solution)/shard_map/scatter_terms/pallas_call | solution.py:337
  80.5 46.6 %mean_over_workers.1 = (f32[64,2048]{1,0:T(8,128)S(1)}, f32[8,8,128]{2,1,0:T(8,128)S(1)}) custom-call(f32[64,2048]{1,0:T(8,128)S(1)} %get-tuple-element.29.merged, f32[8,128]{1,0:T(8,128)S(1)} %get-tuple-element.30.extra), custom_call_target="tpu_custom_call" | custom-call | tf_op jit(solution)/shard_map/mean_over_workers/pallas_call | solution.py:453
  127.2 0.7 reshape_squeeze.3
  127.8 0.6 copy.23
  128.4 0.0 copy-done.5
  128.4 0.0 copy-done.8
  128.4 10.9 %factors.1 = (f32[64,1536]{1,0:T(8,128)}, f32[64,512]{1,0:T(8,128)}, f32[64,1536]{1,0:T(8,128)}, f32[64,512]{1,0:T(8,128)}, f32[32,1536]{1,0:T(8,128)}, /*index=5*/f32[32,512]{1,0:T(8,128)}) custom-call(f32[64,2048]{1,0:T(8,128)S(1)} %get-tuple-element.32.mean, f32[64,2048]{1,0:T(8,128)S(1)} %get-tuple-element.29.merged, f32[32,1536]{1,0:T(8,128)S(1)} %bitcast.32, ...), custom_call_target="tpu_custom_call" | custom-call | tf_op jit(solution)/shard_map/factors/pallas_call | solution.py:524
  (3 shorter events, 0.0 us)
Async XLA Ops:
  0.6 24.8 %copy-start.11 = (f32[512]{0:T(512)S(1)}, f32[512]{0:T(512)}, u32[]{:S(2)}) copy-start(f32[512]{0:T(512)} %param.16) | copy-start | bytes 6148
  0.7 24.8 %copy-start.10 = (s32[2,144]{1,0:T(2,128)S(1)}, s32[2,144]{1,0:T(2,128)}, u32[]{:S(2)}) copy-start(s32[2,144]{1,0:T(2,128)} %region_ref.1) | copy-start | bytes 3460
  1.4 0.9 copy-start
  2.3 23.1 %copy-start.1 = (s32[144,144]{1,0:T(8,128)S(1)}, s32[144,144]{1,0:T(8,128)}, u32[]{:S(2)}) copy-start(s32[144,144]{1,0:T(8,128)} %bucket_ref.3) | copy-start | bytes 248836
  2.3 23.1 %copy-start.3 = (bf16[2,144,512]{2,1,0:T(8,128)(2,1)S(1)}, bf16[2,144,512]{2,1,0:T(8,128)(2,1)}, u32[]{:S(2)}) copy-start(bf16[2,144,512]{2,1,0:T(8,128)(2,1)} %param.12) | copy-start | bytes 884740
  2.3 23.1 %copy-start.4 = (bf16[2,144,512]{2,1,0:T(8,128)(2,1)S(1)}, bf16[2,144,512]{2,1,0:T(8,128)(2,1)}, u32[]{:S(2)}) copy-start(bf16[2,144,512]{2,1,0:T(8,128)(2,1)} %param.13) | copy-start | bytes 884740
  5.8 0.9 copy-start.6
  6.7 0.8 copy-start.9
  25.5 36.2 %copy-start.2 = (f32[1,64,1536]{2,1,0:T(8,128)S(1)}, f32[1,64,1536]{2,1,0:T(8,128)}, u32[]{:S(2)}) copy-start(f32[1,64,1536]{2,1,0:T(8,128)} %param.20) | copy-start | bytes 1179652
  25.5 36.2 %copy-start.7 = (f32[1,64,512]{2,1,0:T(8,128)S(1)}, f32[1,64,512]{2,1,0:T(8,128)}, u32[]{:S(2)}) copy-start(f32[1,64,512]{2,1,0:T(8,128)} %param.21) | copy-start | bytes 393220
  61.7 66.7 %copy-start.5 = (f32[1,1536,32]{1,2,0:T(8,128)S(1)}, f32[1,1536,32]{1,2,0:T(8,128)}, u32[]{:S(2)}) copy-start(f32[1,1536,32]{1,2,0:T(8,128)} %param.22) | copy-start | bytes 589828
  61.7 66.7 %copy-start.8 = (f32[1,512,32]{1,2,0:T(8,128)S(1)}, f32[1,512,32]{1,2,0:T(8,128)}, u32[]{:S(2)}) copy-start(f32[1,512,32]{1,2,0:T(8,128)} %param.23) | copy-start | bytes 196612

commit v2 on v1

v2 whole, which is shorter than its diff:
```python
import functools

import jax
import jax.numpy as jnp
from jax import lax
from jax.experimental import pallas as pl
from jax.experimental.pallas import tpu as pltpu
from jax.sharding import PartitionSpec as P

NORM_EPS = 1e-05
BASIS_EPS = 1e-06
MASKED = -1e30
HIGH = lax.Precision.HIGHEST
MESH = pl.DeviceIdType.MESH
F32 = jnp.float32
BF16 = jnp.bfloat16
VMEM = pl.BlockSpec(memory_space=pltpu.VMEM)

WIN, SPAN, WIDTH, HEADS, CHUNKS = 2, 144, 512, 8, 6
ROWS = WIN * SPAN
N_X, N_Y, N_Z, N_MP = 4, 4, 16, 8
BLOCK = 64
COLS = 4 * WIDTH


def nt(a, b, **kw):
    return lax.dot_general(a, b, (((1,), (1,)), ((), ())), preferred_element_type=F32, **kw)


def tn(a, b, **kw):
    return lax.dot_general(a, b, (((0,), (0,)), ((), ())), preferred_element_type=F32, **kw)


def nn(a, b, **kw):
    return jnp.dot(a, b, preferred_element_type=F32, **kw)


def gather_kernel(in_ref, out_ref, full_in, full_out, send, recv, fsend, frecv, local):
    mp = lax.axis_index("mp")
    x, core = mp // 2, mp % 2
    sibling = {"mp": 2 * x + 1 - core}

    def peer(step):
        return {"mp": 2 * ((x + step) % N_X) + core}

    barrier = pltpu.get_barrier_semaphore()
    for target in (sibling, peer(1), peer(2), peer(3)):
        pl.semaphore_signal(barrier, inc=1, device_id=target, device_id_type=MESH)

    def rows(index):
        return pl.ds(pl.multiple_of(index * BLOCK, BLOCK), BLOCK)

    arrays = ((in_ref, full_in), (out_ref, full_out))
    own = [pltpu.make_async_copy(src, full.at[rows(mp)], local.at[k]) for k, (src, full) in enumerate(arrays)]
    for copy in own:
        copy.start()
    pl.semaphore_wait(barrier, 4)

    first = {}
    for step in (2, 1, 3):
        for k, (src, full) in enumerate(arrays):
            first[step, k] = pltpu.make_async_remote_copy(
                src, full.at[rows(mp)], send.at[k, step - 1], recv.at[k, step - 1], device_id=peer(step), device_id_type=MESH
            )
            first[step, k].start()
    forward = []
    for k, (src, full) in enumerate(arrays):
        copy = pltpu.make_async_remote_copy(
            src, full.at[rows(mp)], fsend.at[k, 0], frecv.at[k, 0], device_id=sibling, device_id_type=MESH
        )
        copy.start()
        forward.append(copy)
    for k in range(2):
        for step in (1, 3, 2):
            full = arrays[k][1]
            first[step, k].wait_recv()
            slab = full.at[rows(2 * ((x + N_X - step) % N_X) + core)]
            copy = pltpu.make_async_remote_copy(
                slab, slab, fsend.at[k, step], frecv.at[k, step], device_id=sibling, device_id_type=MESH
            )
            copy.start()
            forward.append(copy)
    for copy in own:
        copy.wait()
    for copy in first.values():
        copy.wait_send()
    for copy in forward:
        copy.wait()


def gather_weights(in_weight, out_weight):
    return pl.pallas_call(
        gather_kernel,
        out_shape=(
            jax.ShapeDtypeStruct((WIDTH, 3 * WIDTH), BF16),
            jax.ShapeDtypeStruct((WIDTH, WIDTH), BF16),
        ),
        in_specs=[VMEM, VMEM],
        out_specs=(VMEM, VMEM),
        scratch_shapes=[
            pltpu.SemaphoreType.DMA((2, 3)),
            pltpu.SemaphoreType.DMA((2, 3)),
            pltpu.SemaphoreType.DMA((2, 4)),
            pltpu.SemaphoreType.DMA((2, 4)),
            pltpu.SemaphoreType.DMA((2,)),
        ],
        compiler_params=pltpu.CompilerParams(collective_id=0, has_side_effects=True, vmem_limit_bytes=32 << 20),
        name="gather_weights",
    )(in_weight, out_weight)


def bias_kernel(table_ref, bucket_ref, bias_ref, wide):
    wide[...] = jnp.zeros_like(wide)
    wide[:, :SPAN] = bucket_ref[...]
    for part in range(2):
        lanes = 128 if part == 0 else SPAN - 128
        start = part * 128

        @pl.loop(0, SPAN // 16)
        def _(block):
            at = pl.ds(pl.multiple_of(block * 16, 16), 16)
            index = wide[at, pl.ds(start, 128)]
            low = index & 127
            chunk = index >> 7
            for head in range(HEADS):
                found = jnp.zeros((16, 128), F32)
                for c in range(CHUNKS):
                    row = jnp.broadcast_to(table_ref[head : head + 1, c * 128 : (c + 1) * 128], (16, 128))
                    found = jnp.where(chunk == c, jnp.take_along_axis(row, low, axis=1), found)
                bias_ref[head, at, start : start + lanes] = found[:, :lanes]


def bias_lookup(table, bucket):
    return pl.pallas_call(
        bias_kernel,
        out_shape=jax.ShapeDtypeStruct((HEADS, SPAN, SPAN), F32),
        in_specs=[VMEM, VMEM],
        out_specs=VMEM,
        scratch_shapes=[pltpu.VMEM((SPAN, 256), jnp.int32)],
        compiler_params=pltpu.CompilerParams(vmem_limit_bytes=32 << 20),
        name="bias_lookup",
    )(table, bucket)


def layer_kernel(
    tok_ref, cot_ref, region_ref, bucket_ref, bias_ref, gain_ref, win_ref, wout_ref, in_error, out_error,
    tokgrad_ref, merged, mean, extra_all,
    proj, mixgrad, mixed, packed, normed, x_hat, score_high, score_low,
    prod, near, mine, far,
    err_y, err_slab, err_z, err_full,
    sum_src, sum_y, sum_slab, sum_z, sum_full,
    ex, ex_near, ex_mine, ex_far, ex_part, ex_y, ex_z,
    s_near, r_near, s_far, r_far,
    s_ey, r_ey, s_ez, r_ez, s_ezz, r_ezz, s_eyy, r_eyy,
    s_ty, r_ty, s_tz, r_tz, s_tzz, r_tzz, s_tyy, r_tyy,
    s_xn, r_xn, s_xf, r_xf, s_xy, r_xy, s_xz, r_xz, s_xx, r_xx, s_xs, r_xs,
):
    dp, mp = lax.axis_index("dp"), lax.axis_index("mp")
    z, y, x, core = dp // N_Y, dp % N_Y, mp // 2, mp % 2
    sibling = {"mp": 2 * x + 1 - core}
    split = 3 * WIDTH

    def x_peer(step):
        return {"mp": 2 * ((x + step) % N_X) + core}

    def y_peer(step):
        return {"dp": z * N_Y + (y + step) % N_Y}

    def z_peer(step):
        return {"dp": ((z + step) % N_Z) * N_Y + y}

    sent = []

    def remote(src, dst, send, recv, target):
        copy = pltpu.make_async_remote_copy(src, dst, send, recv, device_id=target, device_id_type=MESH)
        copy.start()
        sent.append(copy)
        return copy

    def slab_rows(index):
        return pl.ds(pl.multiple_of(index * 16, 16), 16)

    four = (2, 1, 3)
    z_steps = (8, 7, 9, 6, 10, 5, 11, 4, 12, 3, 13, 2, 14, 1, 15)
    near_first = tuple(reversed(z_steps))

    barrier = pltpu.get_barrier_semaphore()
    peers = [z_peer(s) for s in z_steps] + [y_peer(s) for s in four] + [x_peer(s) for s in four] + [sibling]
    for target in peers:
        pl.semaphore_signal(barrier, inc=1, device_id=target, device_id_type=MESH)

    gain = gain_ref[...]
    wide = tok_ref[...].astype(F32)
    centered = wide - jnp.mean(wide, axis=-1, keepdims=True)
    inv_sigma = lax.rsqrt(jnp.mean(centered * centered, axis=-1, keepdims=True) + NORM_EPS)
    x_hat[...] = centered * inv_sigma
    normed[...] = (x_hat[...] * gain).astype(BF16)
    proj[...] = nn(normed[...], win_ref[...]).astype(BF16)
    mixgrad[...] = nt(cot_ref[...], wout_ref[...]).astype(BF16)

    pl.semaphore_wait(barrier, len(peers))

    e_y = []
    for s in four:
        rows = slab_rows((y + s) % N_Y)
        e_y.append(remote(in_error.at[rows], err_y.at[s, :, pl.ds(0, split)], s_ey.at[s, 0], r_ey.at[s, 0], y_peer(s)))
        e_y.append(
            remote(out_error.at[rows], err_y.at[s, :, pl.ds(split, WIDTH)], s_ey.at[s, 1], r_ey.at[s, 1], y_peer(s))
        )

    lane = lax.broadcasted_iota(jnp.int32, (1, 128), 1)
    first_half = lane < 64
    halves = (first_half.astype(BF16), (lane >= 64).astype(BF16))
    scale = jnp.asarray(0.125, BF16)
    allowed = []
    for w in range(WIN):
        square = jnp.broadcast_to(region_ref[w : w + 1, :].astype(F32), (SPAN, SPAN))
        allowed.append(square == square.T)

    @pl.loop(0, HEADS // 2)
    def _(pair):
        at = [pl.ds(pl.multiple_of(k * WIDTH + pair * 128, 128), 128) for k in range(3)]
        grads = [[], []]
        for w in range(WIN):
            rows = pl.ds(w * SPAN, SPAN)
            q = proj[rows, at[0]] * scale
            key = proj[rows, at[1]]
            value = proj[rows, at[2]]
            key_scaled = key * scale
            grad = mixgrad[rows, at[0]]
            parts = []
            for t in range(2):
                scores = nt(q * halves[t], key) + bias_ref[2 * pair + t]
                scores = jnp.where(allowed[w], scores, MASKED)
                exps = jnp.exp(scores - jnp.max(scores, axis=-1, keepdims=True))
                prob = exps * (1.0 / jnp.sum(exps, axis=-1, keepdims=True))
                prob_b = prob.astype(BF16)
                out = nn(prob_b, value)
                prob_grad = nt(grad * halves[t], value)
                value_grad = tn(prob_b, grad)
                score_grad = prob * (prob_grad - jnp.sum(prob * prob_grad, axis=-1, keepdims=True))
                grads[t].append(score_grad)
                score_b = score_grad.astype(BF16)
                parts.append((nn(score_b, key_scaled), tn(score_b, q), value_grad, out))
            joined = [jnp.where(first_half, a, b).astype(BF16) for a, b in zip(*parts)]
            for k in range(3):
                packed[rows, at[k]] = joined[k]
            mixed[rows, at[0]] = joined[3]
        for t in range(2):
            total = grads[t][0] + grads[t][1]
            high = total.astype(BF16).astype(F32)
            score_high[2 * pair + t] = high
            score_low[2 * pair + t] = total - high

    first = {}
    for s in (2, 1, 3, 0):
        cols = pl.ds(pl.multiple_of(((x + s) % N_X) * 128, 128), 128)
        prod[s, :, :split] = tn(normed[:, cols], packed[...]).astype(BF16)
        prod[s, :, split:] = tn(mixed[:, cols], cot_ref[...]).astype(BF16)
        other = pl.ds(pl.multiple_of((1 - core) * BLOCK, BLOCK), BLOCK)
        first[s] = remote(prod.at[s, other], near.at[s], s_near.at[s], r_near.at[s], sibling)
    own = pl.ds(pl.multiple_of(core * BLOCK, BLOCK), BLOCK)
    second = {}

    def send_second(s, c):
        rows = slab_rows((y + c) % N_Y)
        second[s, c] = remote(mine.at[s, rows], far.at[s, rows], s_far.at[s, c], r_far.at[s, c], x_peer(s))

    for s in four:
        first[s].wait_recv()
        mine[s] = (prod[s, own].astype(F32) + near[s].astype(F32)).astype(BF16)
        if s == 2:
            for c in (2, 1, 3, 0):
                send_second(s, c)
    for c in (2, 1, 3, 0):
        send_second(1, c)
        send_second(3, c)
    first[0].wait_recv()
    merged[...] = prod[0, own].astype(F32) + near[0].astype(F32)

    for copy in e_y:
        copy.wait_recv()
    err = err_y[1] + err_y[2] + err_y[3]
    err_in = err[:, :split] + in_error[slab_rows(y), :]
    err_out = err[:, split:] + out_error[slab_rows(y), :]
    for k in range(N_Z):
        src = err_in if k < 12 else err_out
        err_slab[k] = src[:, 128 * (k % 12) : 128 * (k % 12) + 128]
    e_z = {s: remote(err_slab.at[(z + s) % N_Z], err_z.at[s], s_ez.at[s], r_ez.at[s], z_peer(s)) for s in z_steps}

    normed_grad = nt(packed[...], win_ref[...])
    gain_term = jnp.sum(normed_grad * x_hat[...], axis=0, keepdims=True)
    hat_grad = normed_grad * gain
    delta = inv_sigma * (
        hat_grad
        - jnp.mean(hat_grad, axis=-1, keepdims=True)
        - x_hat[...] * jnp.mean(hat_grad * x_hat[...], axis=-1, keepdims=True)
    )
    tokgrad_ref[...] = (cot_ref[...].astype(F32) + delta).astype(BF16)

    chunk_row = lax.broadcasted_iota(jnp.int32, (8, SPAN), 0)
    within = lax.broadcasted_iota(jnp.int32, (128, SPAN), 0)

    def add_rows(block, total):
        for k in range(8):
            i = block * 8 + k
            bucket = bucket_ref[pl.ds(i, 1), :]
            chunk_is = jnp.broadcast_to(bucket >> 7, (8, SPAN)) == chunk_row
            one_hot = jnp.where(jnp.broadcast_to(bucket & 127, (128, SPAN)) == within, 1.0, 0.0).astype(BF16)
            picked = jnp.concatenate(
                [
                    jnp.where(chunk_is, jnp.broadcast_to(part[head, pl.ds(i, 1), :], (8, SPAN)), 0.0)
                    for part in (score_high, score_low)
                    for head in range(HEADS)
                ],
                axis=0,
            ).astype(BF16)
            total = total + nt(picked, one_hot)
        return total

    total = lax.fori_loop(0, SPAN // 8, add_rows, jnp.zeros((128, 128), F32))
    table_term = total[:64] + total[64:]
    for head in range(HEADS):
        ex[head // 2, head % 2] = table_term[8 * head : 8 * head + 8]
        part = gain_term[:, 128 * (head // 2) : 128 * (head // 2 + 1)]
        if head % 2:
            part = pltpu.roll(part, 64, 1)
        ex[head // 2, head % 2, 6:7, :] = part
    x_near = {
        s: remote(ex.at[(x + s) % N_X, 1 - core], ex_near.at[s], s_xn.at[s], r_xn.at[s], sibling) for s in (2, 1, 3, 0)
    }

    piece = err_slab[z]
    for s in near_first:
        e_z[s].wait_recv()
        piece = piece + err_z[s]
    err_full[y, z] = piece * (1.0 / (N_Y * N_Z))
    here = err_full.at[y, z]
    e_zz = {s: remote(here, here, s_ezz.at[s], r_ezz.at[s], z_peer(s)) for s in z_steps}

    t_y = {}
    x_far = {}
    for c in (2, 1, 3, 0):
        rows = slab_rows((y + c) % N_Y)
        for s in (1, 3, 2):
            second[s, c].wait_recv()
        total = merged[rows, :] + far[1, rows].astype(F32) + far[3, rows].astype(F32) + far[2, rows].astype(F32)
        total = total * (1.0 / N_MP)
        merged[rows, :split] = total[:, :split] + in_error[rows, :]
        merged[rows, split:] = total[:, split:] + out_error[rows, :]
        if c:
            sum_src[rows, :] = total.astype(BF16)
            t_y[c] = remote(sum_src.at[rows], sum_y.at[c], s_ty.at[c], r_ty.at[c], y_peer(c))
        if c == 2:
            for s in four:
                x_near[s].wait_recv()
                ex_mine[s] = ex[(x + s) % N_X, core] + ex_near[s]
                x_far[s] = remote(ex_mine.at[s], ex_far.at[s], s_xf.at[s], r_xf.at[s], x_peer(s))
    for s in four:
        t_y[s].wait_recv()
        total = total + sum_y[s].astype(F32)
    for k in range(N_Z):
        sum_slab[k] = total[:, 128 * k : 128 * (k + 1)]
    rounded = sum_slab[...].astype(BF16)
    sum_send = sum_full.at[N_Y]
    sum_full[N_Y] = rounded
    t_z = {s: remote(sum_send.at[(z + s) % N_Z], sum_z.at[s], s_tz.at[s], r_tz.at[s], z_peer(s)) for s in z_steps}

    x_near[0].wait_recv()
    part = ex[x, core] + ex_near[0]
    for s in four:
        x_far[s].wait_recv()
        part = part + ex_far[s]
    ex_part[0] = part
    x_y = {s: remote(ex_part.at[0], ex_y.at[s], s_xy.at[s], r_xy.at[s], y_peer(s)) for s in four}

    for s in near_first:
        e_zz[s].wait_recv()
    here = err_full.at[y]
    e_yy = {s: remote(here, here, s_eyy.at[s], r_eyy.at[s], y_peer(s)) for s in four}

    piece = sum_slab[z]
    for s in near_first:
        t_z[s].wait_recv()
        piece = piece + sum_z[s].astype(F32)
    sum_full[y, z] = (piece * (1.0 / (N_Y * N_Z))).astype(BF16)
    here = sum_full.at[y, z]
    t_zz = {s: remote(here, here, s_tzz.at[s], r_tzz.at[s], z_peer(s)) for s in z_steps}

    for s in four:
        x_y[s].wait_recv()
        part = part + ex_y[s]
    ex_part[1] = part
    x_z = {s: remote(ex_part.at[1], ex_z.at[s], s_xz.at[s], r_xz.at[s], z_peer(s)) for s in z_steps}

    for s in near_first:
        t_zz[s].wait_recv()
    here = sum_full.at[y]
    t_yy = {s: remote(here, here, s_tyy.at[s], r_tyy.at[s], y_peer(s)) for s in four}

    for s in near_first:
        x_z[s].wait_recv()
        part = part + ex_z[s]
    extra_all[mp] = part
    here = extra_all.at[mp]
    x_x = {s: remote(here, here, s_xx.at[s], r_xx.at[s], x_peer(s)) for s in four}
    x_s = [remote(here, here, s_xs.at[0], r_xs.at[0], sibling)]

    def finish(slab):
        for k in range(N_Z):
            mean[slab_rows(slab), 128 * k : 128 * (k + 1)] = err_full[slab, k] + sum_full[slab, k].astype(F32)

    finish(y)
    for s in (1, 3, 2):
        x_x[s].wait_recv()
        here = extra_all.at[2 * ((x + N_X - s) % N_X) + core]
        x_s.append(remote(here, here, s_xs.at[s], r_xs.at[s], sibling))
    for s in (1, 3, 2):
        e_yy[s].wait_recv()
        t_yy[s].wait_recv()
        finish((y + N_Y - s) % N_Y)
    for copy in x_s:
        copy.wait_recv()
    for copy in sent:
        copy.wait_send()


def layer(*operands):
    def vmem(*shape, dtype=F32):
        return pltpu.VMEM(shape, dtype)

    def dma(*shape):
        return [pltpu.SemaphoreType.DMA(shape)] * 2

    return pl.pallas_call(
        layer_kernel,
        out_shape=(
            jax.ShapeDtypeStruct((ROWS, WIDTH), BF16),
            jax.ShapeDtypeStruct((BLOCK, COLS), F32),
            jax.ShapeDtypeStruct((BLOCK, COLS), F32),
            jax.ShapeDtypeStruct((N_MP, 8, 128), F32),
        ),
        in_specs=[VMEM] * len(operands),
        out_specs=(VMEM,) * 4,
        scratch_shapes=[
            vmem(ROWS, 3 * WIDTH, dtype=BF16),
            vmem(ROWS, WIDTH, dtype=BF16),
            vmem(ROWS, WIDTH, dtype=BF16),
            vmem(ROWS, 3 * WIDTH, dtype=BF16),
            vmem(ROWS, WIDTH, dtype=BF16),
            vmem(ROWS, WIDTH),
            vmem(HEADS, SPAN, SPAN),
            vmem(HEADS, SPAN, SPAN),
            vmem(N_X, 2 * BLOCK, COLS, dtype=BF16),
            vmem(N_X, BLOCK, COLS, dtype=BF16),
            vmem(N_X, BLOCK, COLS, dtype=BF16),
            vmem(N_X, BLOCK, COLS, dtype=BF16),
            vmem(N_Y, 16, COLS),
            vmem(N_Z, 16, 128),
            vmem(N_Z, 16, 128),
            vmem(N_Y, N_Z, 16, 128),
            vmem(BLOCK, COLS, dtype=BF16),
            vmem(N_Y, 16, COLS, dtype=BF16),
            vmem(N_Z, 16, 128),
            vmem(N_Z, 16, 128, dtype=BF16),
            vmem(N_Y + 1, N_Z, 16, 128, dtype=BF16),
            vmem(N_X, 2, 8, 128),
            vmem(N_X, 8, 128),
            vmem(N_X, 8, 128),
            vmem(N_X, 8, 128),
            vmem(2, 8, 128),
            vmem(N_Y, 8, 128),
            vmem(N_Z, 8, 128),
        ]
        + dma(4) + dma(4, 4)
        + dma(4, 2) + dma(N_Z) + dma(N_Z) + dma(4)
        + dma(4) + dma(N_Z) + dma(N_Z) + dma(4)
        + dma(4) + dma(4) + dma(4) + dma(N_Z) + dma(4) + dma(4),
        compiler_params=pltpu.CompilerParams(collective_id=1, has_side_effects=True, vmem_limit_bytes=48 << 20),
        name="layer",
    )(*operands)


def factor_kernel(
    mean, merged, in_basis, out_basis, in_update, out_update, in_error, out_error, in_right, out_right, left
):
    split = 3 * WIDTH
    left[:, :BLOCK] = nt(in_basis[...], mean[:, :split], precision=HIGH)
    left[:, BLOCK:] = nt(out_basis[...], mean[:, split:], precision=HIGH)

    lane = lax.broadcasted_iota(jnp.int32, (8, 128), 1)
    row = lax.broadcasted_iota(jnp.int32, (8, 128), 0)
    is_in = lane < BLOCK

    def half_sums(a):
        in_sum = jnp.sum(jnp.where(is_in, a, 0.0), axis=1, keepdims=True)
        out_sum = jnp.sum(jnp.where(is_in, 0.0, a), axis=1, keepdims=True)
        return jnp.where(is_in, in_sum, out_sum)

    finished = []
    for c in range(32):
        column = jnp.broadcast_to(left[c : c + 1, :], (8, 128))
        if c:
            for _ in range(2):
                taken = None
                for group in finished:
                    term = group * half_sums(group * column)
                    taken = term if taken is None else taken + term
                column = column - jnp.sum(taken, axis=0, keepdims=True)
        column = column * lax.rsqrt(half_sums(column * column) + BASIS_EPS)
        if c % 8 == 0:
            finished.append(jnp.where(row == 0, column, 0.0))
        else:
            finished[-1] = jnp.where(row == c % 8, column, finished[-1])
    ortho = jnp.concatenate(finished, axis=0)
    in_ortho, out_ortho = ortho[:, :BLOCK], ortho[:, BLOCK:]
    right = nn(in_ortho, mean[:, :split], precision=HIGH)
    in_right[...] = right
    update = tn(in_ortho, right, precision=HIGH)
    in_update[...] = update
    in_error[...] = merged[:, :split] - update
    right = nn(out_ortho, mean[:, split:], precision=HIGH)
    out_right[...] = right
    update = tn(out_ortho, right, precision=HIGH)
    out_update[...] = update
    out_error[...] = merged[:, split:] - update


def factors(mean, merged, in_basis, out_basis):
    wide = jax.ShapeDtypeStruct((BLOCK, 3 * WIDTH), F32)
    thin = jax.ShapeDtypeStruct((BLOCK, WIDTH), F32)
    return pl.pallas_call(
        factor_kernel,
        out_shape=(
            wide, thin, wide, thin,
            jax.ShapeDtypeStruct((32, 3 * WIDTH), F32),
            jax.ShapeDtypeStruct((32, WIDTH), F32),
        ),
        in_specs=[VMEM] * 4,
        out_specs=(VMEM,) * 6,
        scratch_shapes=[pltpu.VMEM((32, 128), F32)],
        compiler_params=pltpu.CompilerParams(vmem_limit_bytes=32 << 20),
        name="factors",
    )(mean, merged, in_basis, out_basis)


def shards(
    tokens,
    cotangent,
    region_ids,
    rel_bucket,
    norm_gain,
    in_weight,
    out_weight,
    bias_table,
    in_error,
    out_error,
    in_basis,
    out_basis,
):
    devices = lax.axis_size("dp") * lax.axis_size("mp")
    buckets = bias_table.shape[1]
    full_in, full_out = gather_weights(in_weight, out_weight)
    table = jnp.pad(bias_table, ((0, 0), (0, CHUNKS * 128 - buckets)))
    bias = bias_lookup(table, rel_bucket)
    token_grad, merged, mean, extra_all = layer(
        tokens.reshape(ROWS, WIDTH), cotangent.reshape(ROWS, WIDTH), region_ids, rel_bucket, bias,
        norm_gain.reshape(1, WIDTH), full_in, full_out, in_error[0], out_error[0],
    )
    in_update, out_update, in_new, out_new, in_right, out_right = factors(
        mean, merged, in_basis[0].T, out_basis[0].T
    )
    extra_all = extra_all * (1.0 / devices)
    gain_grad = extra_all[:, 6, :64].reshape(WIDTH)
    table_grad = extra_all[:, :CHUNKS, :].reshape(HEADS, CHUNKS * 128)[:, :buckets]
    return (
        token_grad.reshape(tokens.shape),
        gain_grad,
        table_grad,
        in_update,
        out_update,
        in_new[None],
        out_new[None],
        in_right.T[None],
        out_right.T[None],
    )


def solution(mesh):
    placed = (
        P(("dp", "mp"), None, None),
        P(("dp", "mp"), None, None),
        P(("dp", "mp"), None),
        P(),
        P(),
        P("mp", None),
        P("mp", None),
        P(),
        P("dp", "mp", None),
        P("dp", "mp", None),
        P("mp", None, None),
        P("mp", None, None),
    )
    return jax.shard_map(
        shards,
        mesh=mesh,
        in_specs=placed,
        out_specs=(
            P(("dp", "mp"), None, None),
            P(),
            P(),
            P("mp", None),
            P("mp", None),
            P("dp", "mp", None),
            P("dp", "mp", None),
            P("mp", None, None),
            P("mp", None, None),
        ),
        check_vma=False,
    )
```

time: 140 us -> 106 us (0.76)
  the two profiles are of different devices: /device:TPU:8 before, /device:TPU:1 now
where the time goes in v2:
time: 106 us; the launch traced here: 105 us
  Pallas kernels  99.1 us (93%)
  local copies, waits for them, and re-layouts  5.47 us (5%)
    pallas_call x1, Pallas kernels, layer(): pl.pallas_call(layer_kernel, out_shape=(jax.ShapeDtypeStruct((ROWS, WIDTH...  65.4 us
    pallas_call x1, Pallas kernels, gather_weights(): pl.pallas_call(gather_kernel, out_shape=(jax.ShapeDtypeStruct((WIDTH, 3 *...  19.4 us
    pallas_call x1, Pallas kernels, factors(): pl.pallas_call(factor_kernel, out_shape=(wide, thin, wide, thin, jax.Shap...  10.9 us
    unnamed x27, local copies, waits for them, and re-layouts  4.04 us
    pallas_call x1, Pallas kernels, bias_lookup(): pl.pallas_call(bias_kernel, out_shape=jax.ShapeDtypeStruct((HEADS, SPAN,...  3.43 us

profile of v2, /device:TPU:1, one launch (start us, length us, event | category | flops | bytes accessed | tf_op | source)
XLA Modules:
  0.0 105.4 jit_solution(3434390246918867503)
XLA Ops:
  0.6 0.0 copy-start.11
  0.7 0.0 copy-start.10
  0.7 0.8 pad.4.table_ref
  1.4 0.0 copy-start
  1.4 0.9 copy-done
  2.3 0.0 copy-start.1
  2.3 0.0 copy-start.2
  2.3 0.0 copy-start.3
  2.3 0.0 copy-start.4
  2.3 0.0 copy-start.7
  2.4 3.4 %bias_lookup.1.bias_ref = f32[8,144,144]{2,1,0:T(8,128)S(1)} custom-call(f32[8,768]{1,0:T(8,128)S(1)} %pad.4.table_ref, s32[144,144]{1,0:T(8,128)S(1)} %copy-done), custom_call_target="tpu_custom_call" | custom-call | tf_op jit(solution)/shard_map/bias_lookup/pallas_call | solution.py:134
  5.8 0.0 copy-start.6
  5.8 0.9 copy-done.6
  6.7 0.0 copy-start.9
  6.7 0.8 copy-done.9
  7.6 19.4 %gather_weights.1 = (bf16[512,1536]{1,0:T(8,128)(2,1)S(1)}, bf16[512,512]{1,0:T(8,128)(2,1)S(1)}) custom-call(bf16[64,1536]{1,0:T(8,128)(2,1)S(1)} %copy-done.6, bf16[64,512]{1,0:T(8,128)(2,1)S(1)} %copy-done.9), custom_call_target="tpu_custom_call" | custom-call | tf_op jit(solution)/shard_map/gather_weights/pallas_call | solution.py:92
  26.9 0.0 copy-done.11
  26.9 0.0 copy-done.10
  27.0 0.0 copy-done.1
  27.0 0.0 copy-done.2
  27.0 0.0 copy-done.3
  27.0 0.0 copy-done.4
  27.0 0.0 copy-done.7
  27.0 0.0 copy-start.5
  27.0 0.0 copy-start.8
  27.0 65.4 %layer.1 = (bf16[288,512]{1,0:T(8,128)(2,1)S(1)}, f32[64,2048]{1,0:T(8,128)S(1)}, f32[64,2048]{1,0:T(8,128)S(1)}, f32[8,8,128]{2,1,0:T(8,128)S(1)}) custom-call(bf16[288,512]{1,0:T(8,128)(2,1)S(1)} %bitcast.28, bf16[288,512]{1,0:T(8,128)(2,1)S(1)} %bitcast.29, s32[2,144]{1,0:T(2,128)S(1)} %copy-done.10, s32[144,144]{1,0:T(8,128)S(1)} %copy-done.1, ...), custom_call_target="tpu_custom_call" | custom-call | tf_op jit(solution)/shard_map/layer/pallas_call | solution.py:435
  92.5 0.7 reshape_squeeze.3
  93.2 0.6 copy.23
  93.8 0.0 copy-done.5
  93.8 0.0 copy-done.8
  93.8 10.9 %factors.1 = (f32[64,1536]{1,0:T(8,128)}, f32[64,512]{1,0:T(8,128)}, f32[64,1536]{1,0:T(8,128)}, f32[64,512]{1,0:T(8,128)}, f32[32,1536]{1,0:T(8,128)}, /*index=5*/f32[32,512]{1,0:T(8,128)}) custom-call(f32[64,2048]{1,0:T(8,128)S(1)} %get-tuple-element.25.mean, f32[64,2048]{1,0:T(8,128)S(1)} %get-tuple-element.26.merged, f32[32,1536]{1,0:T(8,128)S(1)} %bitcast.30, ...), custom_call_target="tpu_custom_call" | custom-call | tf_op jit(solution)/shard_map/factors/pallas_call | solution.py:532
  104.7 0.7 copy.25
  (3 shorter events, 0.0 us)
Async XLA Ops:
  0.6 26.3 %copy-start.11 = (f32[512]{0:T(512)S(1)}, f32[512]{0:T(512)}, u32[]{:S(2)}) copy-start(f32[512]{0:T(512)} %param.16) | copy-start | bytes 6148
  0.7 26.3 %copy-start.10 = (s32[2,144]{1,0:T(2,128)S(1)}, s32[2,144]{1,0:T(2,128)}, u32[]{:S(2)}) copy-start(s32[2,144]{1,0:T(2,128)} %region_ref.1) | copy-start | bytes 3460
  1.4 0.9 copy-start
  2.3 24.6 %copy-start.1 = (s32[144,144]{1,0:T(8,128)S(1)}, s32[144,144]{1,0:T(8,128)}, u32[]{:S(2)}) copy-start(s32[144,144]{1,0:T(8,128)} %bucket_ref.3) | copy-start | bytes 248836
  2.3 24.6 %copy-start.2 = (f32[1,64,1536]{2,1,0:T(8,128)S(1)}, f32[1,64,1536]{2,1,0:T(8,128)}, u32[]{:S(2)}) copy-start(f32[1,64,1536]{2,1,0:T(8,128)} %param.20) | copy-start | bytes 1179652
  2.3 24.6 %copy-start.3 = (bf16[2,144,512]{2,1,0:T(8,128)(2,1)S(1)}, bf16[2,144,512]{2,1,0:T(8,128)(2,1)}, u32[]{:S(2)}) copy-start(bf16[2,144,512]{2,1,0:T(8,128)(2,1)} %param.12) | copy-start | bytes 884740
  2.3 24.7 %copy-start.4 = (bf16[2,144,512]{2,1,0:T(8,128)(2,1)S(1)}, bf16[2,144,512]{2,1,0:T(8,128)(2,1)}, u32[]{:S(2)}) copy-start(bf16[2,144,512]{2,1,0:T(8,128)(2,1)} %param.13) | copy-start | bytes 884740
  2.3 24.7 %copy-start.7 = (f32[1,64,512]{2,1,0:T(8,128)S(1)}, f32[1,64,512]{2,1,0:T(8,128)}, u32[]{:S(2)}) copy-start(f32[1,64,512]{2,1,0:T(8,128)} %param.21) | copy-start | bytes 393220
  5.8 0.9 copy-start.6
  6.7 0.8 copy-start.9
  27.0 66.8 %copy-start.5 = (f32[1,1536,32]{1,2,0:T(8,128)S(1)}, f32[1,1536,32]{1,2,0:T(8,128)}, u32[]{:S(2)}) copy-start(f32[1,1536,32]{1,2,0:T(8,128)} %param.22) | copy-start | bytes 589828
  27.0 66.8 %copy-start.8 = (f32[1,512,32]{1,2,0:T(8,128)S(1)}, f32[1,512,32]{1,2,0:T(8,128)}, u32[]{:S(2)}) copy-start(f32[1,512,32]{1,2,0:T(8,128)} %param.23) | copy-start | bytes 196612

commit v3 on v2

--- a/solution.py
+++ b/solution.py
@@ -1,5 +1,3 @@
-import functools
-
 import jax
 import jax.numpy as jnp
 from jax import lax
@@ -15,6 +13,7 @@
 F32 = jnp.float32
 BF16 = jnp.bfloat16
 VMEM = pl.BlockSpec(memory_space=pltpu.VMEM)
+HBM = pl.BlockSpec(memory_space=pltpu.HBM)
 
 WIN, SPAN, WIDTH, HEADS, CHUNKS = 2, 144, 512, 8, 6
 ROWS = WIN * SPAN
@@ -35,117 +34,150 @@
     return jnp.dot(a, b, preferred_element_type=F32, **kw)
 
 
-def gather_kernel(in_ref, out_ref, full_in, full_out, send, recv, fsend, frecv, local):
+def gather_kernel(
+    in_ref, out_ref, table_hbm, bucket_hbm, tok_hbm, gain_hbm,
+    full_in, full_out, bias_ref, normed_ref,
+    table_ref, bucket_ref, tok_ref, gain_ref, index, table, send, recv, rsend, rrecv, fsend, frecv, local,
+):
     mp = lax.axis_index("mp")
     x, core = mp // 2, mp % 2
     sibling = {"mp": 2 * x + 1 - core}
 
-    def peer(step):
-        return {"mp": 2 * ((x + step) % N_X) + core}
-
+    def device(step):
+        return 2 * ((x + step) % N_X) + core
+
+    right, left = {"mp": device(1)}, {"mp": device(3)}
     barrier = pltpu.get_barrier_semaphore()
-    for target in (sibling, peer(1), peer(2), peer(3)):
+    for target in (right, left, sibling):
         pl.semaphore_signal(barrier, inc=1, device_id=target, device_id_type=MESH)
 
-    def rows(index):
-        return pl.ds(pl.multiple_of(index * BLOCK, BLOCK), BLOCK)
-
-    arrays = ((in_ref, full_in), (out_ref, full_out))
-    own = [pltpu.make_async_copy(src, full.at[rows(mp)], local.at[k]) for k, (src, full) in enumerate(arrays)]
-    for copy in own:
+    sources, fulls = (in_ref, out_ref), (full_in, full_out)
+    half_rows = BLOCK // 2
+
+    def rows(owner):
+        return pl.ds(pl.multiple_of(owner * BLOCK, BLOCK), BLOCK)
+
+    def half(owner, h):
+        return pl.ds(pl.multiple_of(owner * BLOCK + h * half_rows, half_rows), half_rows)
+
+    own = [pltpu.make_async_copy(sources[k], fulls[k].at[rows(mp)], local.at[k]) for k in range(2)]
+    staged = [
+        pltpu.make_async_copy(src, dst, local.at[2 + k])
+        for k, (src, dst) in enumerate(
+            ((table_hbm, table_ref), (bucket_hbm, bucket_ref), (tok_hbm, tok_ref), (gain_hbm, gain_ref))
+        )
+    ]
+    for copy in staged + own:
         copy.start()
-    pl.semaphore_wait(barrier, 4)
+    for copy in staged:
+        copy.wait()
+    index[...] = jnp.zeros_like(index)
+    index[:, :SPAN] = bucket_ref[...]
+    table[...] = jnp.zeros_like(table)
+    table[:, : table_ref.shape[1]] = table_ref[...]
+    pl.semaphore_wait(barrier, 3)
+
+    started = []
+
+    def remote(src, dst, send_sem, recv_sem, target):
+        copy = pltpu.make_async_remote_copy(src, dst, send_sem, recv_sem, device_id=target, device_id_type=MESH)
+        copy.start()
+        started.append(copy)
+        return copy
 
     first = {}
-    for step in (2, 1, 3):
-        for k, (src, full) in enumerate(arrays):
-            first[step, k] = pltpu.make_async_remote_copy(
-                src, full.at[rows(mp)], send.at[k, step - 1], recv.at[k, step - 1], device_id=peer(step), device_id_type=MESH
-            )
-            first[step, k].start()
-    forward = []
-    for k, (src, full) in enumerate(arrays):
-        copy = pltpu.make_async_remote_copy(
-            src, full.at[rows(mp)], fsend.at[k, 0], frecv.at[k, 0], device_id=sibling, device_id_type=MESH
-        )
-        copy.start()
-        forward.append(copy)
+    for turn in range(2):
+        for k in range(2):
+            for way, target in ((0, right), (1, left)):
+                h = turn ^ way
+                first[way, k, h] = remote(
+                    sources[k].at[pl.ds(h * half_rows, half_rows)], fulls[k].at[half(mp, h)],
+                    send.at[way, k, h], recv.at[way, k, h], target,
+                )
+    passed = [
+        remote(sources[k], fulls[k].at[rows(mp)], fsend.at[0, k, 0], frecv.at[0, k, 0], sibling) for k in range(2)
+    ]
+
+    def look_up(part):
+        lanes = 128 if part == 0 else SPAN - 128
+
+        @pl.loop(0, SPAN // 16)
+        def _(block):
+            at = pl.ds(pl.multiple_of(block * 16, 16), 16)
+            bucket = index[at, pl.ds(part * 128, 128)]
+            low = bucket & 127
+            chunk = bucket >> 7
+            for head in range(HEADS):
+                found = jnp.zeros((16, 128), F32)
+                for c in range(CHUNKS):
+                    row = jnp.broadcast_to(table[head : head + 1, c * 128 : (c + 1) * 128], (16, 128))
+                    found = jnp.where(chunk == c, jnp.take_along_axis(row, low, axis=1), found)
+                bias_ref[head, at, part * 128 : part * 128 + lanes] = found[:, :lanes]
+
+    def to_sibling(group, k, h, owner):
+        slab = fulls[k].at[half(owner, h)]
+        passed.append(remote(slab, slab, fsend.at[group, k, h], frecv.at[group, k, h], sibling))
+
+    look_up(0)
+    relayed = {}
     for k in range(2):
-        for step in (1, 3, 2):
-            full = arrays[k][1]
-            first[step, k].wait_recv()
-            slab = full.at[rows(2 * ((x + N_X - step) % N_X) + core)]
-            copy = pltpu.make_async_remote_copy(
-                slab, slab, fsend.at[k, step], frecv.at[k, step], device_id=sibling, device_id_type=MESH
-            )
-            copy.start()
-            forward.append(copy)
+        for way, target in ((0, right), (1, left)):
+            h = way
+            first[way, k, h].wait_recv()
+            owner = device(3 if way == 0 else 1)
+            slab = fulls[k].at[half(owner, h)]
+            relayed[way, k] = remote(slab, slab, rsend.at[way, k], rrecv.at[way, k], target)
+            to_sibling(1 + way, k, h, owner)
+    look_up(1)
+    wide = tok_ref[...].astype(F32)
+    centered = wide - jnp.mean(wide, axis=-1, keepdims=True)
+    inv_sigma = lax.rsqrt(jnp.mean(centered * centered, axis=-1, keepdims=True) + NORM_EPS)
+    normed_ref[...] = (centered * inv_sigma * gain_ref[...]).astype(BF16)
+    for k in range(2):
+        for way in range(2):
+            first[way, k, 1 - way].wait_recv()
+            to_sibling(1 + way, k, 1 - way, device(3 if way == 0 else 1))
+    for k in range(2):
+        for way in range(2):
+            relayed[way, k].wait_recv()
+            to_sibling(3, k, way, device(2))
     for copy in own:
         copy.wait()
-    for copy in first.values():
+    for copy in passed:
+        copy.wait_recv()
+    for copy in started:
         copy.wait_send()
-    for copy in forward:
-        copy.wait()
-
-
-def gather_weights(in_weight, out_weight):
+
+
+def gather_weights(*operands):
+    def dma(*shape):
+        return [pltpu.SemaphoreType.DMA(shape)] * 2
+
     return pl.pallas_call(
         gather_kernel,
         out_shape=(
             jax.ShapeDtypeStruct((WIDTH, 3 * WIDTH), BF16),
             jax.ShapeDtypeStruct((WIDTH, WIDTH), BF16),
+            jax.ShapeDtypeStruct((HEADS, SPAN, SPAN), F32),
+            jax.ShapeDtypeStruct((ROWS, WIDTH), BF16),
         ),
-        in_specs=[VMEM, VMEM],
-        out_specs=(VMEM, VMEM),
-        scratch_shapes=[
-            pltpu.SemaphoreType.DMA((2, 3)),
-            pltpu.SemaphoreType.DMA((2, 3)),
-            pltpu.SemaphoreType.DMA((2, 4)),
-            pltpu.SemaphoreType.DMA((2, 4)),
-            pltpu.SemaphoreType.DMA((2,)),
-        ],
+        in_specs=[HBM] * len(operands),
+        out_specs=(VMEM,) * 4,
+        scratch_shapes=[pltpu.VMEM(a.shape, a.dtype) for a in operands[2:]]
+        + [pltpu.VMEM((SPAN, 256), jnp.int32), pltpu.VMEM((HEADS, CHUNKS * 128), F32)]
+        + dma(2, 2, 2) + dma(2, 2) + dma(4, 2, 2)
+        + [pltpu.SemaphoreType.DMA((6,))],
         compiler_params=pltpu.CompilerParams(collective_id=0, has_side_effects=True, vmem_limit_bytes=32 << 20),
         name="gather_weights",
-    )(in_weight, out_weight)
-
-
-def bias_kernel(table_ref, bucket_ref, bias_ref, wide):
-    wide[...] = jnp.zeros_like(wide)
-    wide[:, :SPAN] = bucket_ref[...]
-    for part in range(2):
-        lanes = 128 if part == 0 else SPAN - 128
-        start = part * 128
-
-        @pl.loop(0, SPAN // 16)
-        def _(block):
-            at = pl.ds(pl.multiple_of(block * 16, 16), 16)
-            index = wide[at, pl.ds(start, 128)]
-            low = index & 127
-            chunk = index >> 7
-            for head in range(HEADS):
-                found = jnp.zeros((16, 128), F32)
-                for c in range(CHUNKS):
-                    row = jnp.broadcast_to(table_ref[head : head + 1, c * 128 : (c + 1) * 128], (16, 128))
-                    found = jnp.where(chunk == c, jnp.take_along_axis(row, low, axis=1), found)
-                bias_ref[head, at, start : start + lanes] = found[:, :lanes]
-
-
-def bias_lookup(table, bucket):
-    return pl.pallas_call(
-        bias_kernel,
-        out_shape=jax.ShapeDtypeStruct((HEADS, SPAN, SPAN), F32),
-        in_specs=[VMEM, VMEM],
-        out_specs=VMEM,
-        scratch_shapes=[pltpu.VMEM((SPAN, 256), jnp.int32)],
-        compiler_params=pltpu.CompilerParams(vmem_limit_bytes=32 << 20),
-        name="bias_lookup",
-    )(table, bucket)
+    )(*(pltpu.with_memory_space_constraint(a, pltpu.HBM) for a in operands))
 
 
 def layer_kernel(
-    tok_ref, cot_ref, region_ref, bucket_ref, bias_ref, gain_ref, win_ref, wout_ref, in_error, out_error,
+    cot_hbm, region_hbm, in_error_hbm, out_error_hbm, tok_hbm, gain_hbm, bucket_hbm,
+    bias_ref, normed, win_ref, wout_ref,
     tokgrad_ref, merged, mean, extra_all,
-    proj, mixgrad, mixed, packed, normed, x_hat, score_high, score_low,
+    cot_ref, region_ref, in_error, out_error, tok_ref, gain_ref, bucket_ref, staging,
+    proj, mixgrad, mixed, packed, x_hat, score_high, score_low,
     prod, near, mine, far,
     err_y, err_slab, err_z, err_full,
     sum_src, sum_y, sum_slab, sum_z, sum_full,
@@ -189,24 +221,22 @@
     for target in peers:
         pl.semaphore_signal(barrier, inc=1, device_id=target, device_id_type=MESH)
 
-    gain = gain_ref[...]
-    wide = tok_ref[...].astype(F32)
-    centered = wide - jnp.mean(wide, axis=-1, keepdims=True)
-    inv_sigma = lax.rsqrt(jnp.mean(centered * centered, axis=-1, keepdims=True) + NORM_EPS)
-    x_hat[...] = centered * inv_sigma
-    normed[...] = (x_hat[...] * gain).astype(BF16)
+    staged = [
+        pltpu.make_async_copy(src, dst, staging.at[k])
+        for k, (src, dst) in enumerate(
+            (
+                (cot_hbm, cot_ref), (region_hbm, region_ref), (in_error_hbm, in_error), (out_error_hbm, out_error),
+                (tok_hbm, tok_ref), (gain_hbm, gain_ref), (bucket_hbm, bucket_ref),
+            )
+        )
+    ]
+    for copy in staged:
+        copy.start()
+
     proj[...] = nn(normed[...], win_ref[...]).astype(BF16)
+    for copy in staged:
+        copy.wait()
     mixgrad[...] = nt(cot_ref[...], wout_ref[...]).astype(BF16)
-
-    pl.semaphore_wait(barrier, len(peers))
-
-    e_y = []
-    for s in four:
-        rows = slab_rows((y + s) % N_Y)
-        e_y.append(remote(in_error.at[rows], err_y.at[s, :, pl.ds(0, split)], s_ey.at[s, 0], r_ey.at[s, 0], y_peer(s)))
-        e_y.append(
-            remote(out_error.at[rows], err_y.at[s, :, pl.ds(split, WIDTH)], s_ey.at[s, 1], r_ey.at[s, 1], y_peer(s))
-        )
 
     lane = lax.broadcasted_iota(jnp.int32, (1, 128), 1)
     first_half = lane < 64
@@ -252,6 +282,16 @@
             score_high[2 * pair + t] = high
             score_low[2 * pair + t] = total - high
 
+    pl.semaphore_wait(barrier, len(peers))
+
+    e_y = []
+    for s in four:
+        rows = slab_rows((y + s) % N_Y)
+        e_y.append(remote(in_error.at[rows], err_y.at[s, :, pl.ds(0, split)], s_ey.at[s, 0], r_ey.at[s, 0], y_peer(s)))
+        e_y.append(
+            remote(out_error.at[rows], err_y.at[s, :, pl.ds(split, WIDTH)], s_ey.at[s, 1], r_ey.at[s, 1], y_peer(s))
+        )
+
     first = {}
     for s in (2, 1, 3, 0):
         cols = pl.ds(pl.multiple_of(((x + s) % N_X) * 128, 128), 128)
@@ -288,6 +328,11 @@
         err_slab[k] = src[:, 128 * (k % 12) : 128 * (k % 12) + 128]
     e_z = {s: remote(err_slab.at[(z + s) % N_Z], err_z.at[s], s_ez.at[s], r_ez.at[s], z_peer(s)) for s in z_steps}
 
+    gain = gain_ref[...]
+    wide = tok_ref[...].astype(F32)
+    centered = wide - jnp.mean(wide, axis=-1, keepdims=True)
+    inv_sigma = lax.rsqrt(jnp.mean(centered * centered, axis=-1, keepdims=True) + NORM_EPS)
+    x_hat[...] = centered * inv_sigma
     normed_grad = nt(packed[...], win_ref[...])
     gain_term = jnp.sum(normed_grad * x_hat[...], axis=0, keepdims=True)
     hat_grad = normed_grad * gain
@@ -440,14 +485,15 @@
             jax.ShapeDtypeStruct((BLOCK, COLS), F32),
             jax.ShapeDtypeStruct((N_MP, 8, 128), F32),
         ),
-        in_specs=[VMEM] * len(operands),
+        in_specs=[HBM] * 7 + [VMEM] * 4,
         out_specs=(VMEM,) * 4,
-        scratch_shapes=[
+        scratch_shapes=[pltpu.VMEM(a.shape, a.dtype) for a in operands[:7]]
+        + [pltpu.SemaphoreType.DMA((7,))]
+        + [
             vmem(ROWS, 3 * WIDTH, dtype=BF16),
             vmem(ROWS, WIDTH, dtype=BF16),
             vmem(ROWS, WIDTH, dtype=BF16),
             vmem(ROWS, 3 * WIDTH, dtype=BF16),
-            vmem(ROWS, WIDTH, dtype=BF16),
             vmem(ROWS, WIDTH),
             vmem(HEADS, SPAN, SPAN),
             vmem(HEADS, SPAN, SPAN),
@@ -478,41 +524,55 @@
         + dma(4) + dma(4) + dma(4) + dma(N_Z) + dma(4) + dma(4),
         compiler_params=pltpu.CompilerParams(collective_id=1, has_side_effects=True, vmem_limit_bytes=48 << 20),
         name="layer",
-    )(*operands)
+    )(*(pltpu.with_memory_space_constraint(a, pltpu.HBM) for a in operands[:7]), *operands[7:])
+
+
+def orthonormal_rows(left):
+    lane = lax.broadcasted_iota(jnp.int32, (8, 128), 1)
+    row = lax.broadcasted_iota(jnp.int32, (8, 128), 0)
+    is_in = lane < BLOCK
+    zero = jnp.zeros((8, 128), F32)
+
+    def lane_sum(a):
+        return jnp.sum(a, axis=1, keepdims=True)
+
+    columns = [left[8 * g : 8 * g + 8, :] for g in range(4)]
+    in_columns = [jnp.where(is_in, v, 0.0) for v in columns]
+    out_columns = [jnp.where(is_in, 0.0, v) for v in columns]
+    taken = [zero] * 4
+    in_w, out_w, in_wr, out_wr, squares = ([zero] * 4 for _ in range(5))
+    for c in range(32):
+        g, at = c // 8, c % 8
+        here = row == at
+        vector = jnp.broadcast_to((columns[g] - taken[g])[at : at + 1, :], (8, 128))
+        if c:
+            total = None
+            for k in range(g + 1):
+                term = in_wr[k] * lane_sum(in_w[k] * vector) + out_wr[k] * lane_sum(out_w[k] * vector)
+                total = term if total is None else total + term
+            vector = vector - jnp.sum(total, axis=0, keepdims=True)
+        in_v, out_v = jnp.where(is_in, vector, 0.0), jnp.where(is_in, 0.0, vector)
+        square = jnp.where(is_in, lane_sum(in_v * in_v), lane_sum(out_v * out_v))
+        share = 1.0 / (square + BASIS_EPS)
+        in_scaled, out_scaled = in_v * share, out_v * share
+        for k in range(g, 4):
+            taken[k] = (
+                taken[k] + in_scaled * lane_sum(in_columns[k] * vector) + out_scaled * lane_sum(out_columns[k] * vector)
+            )
+        in_w[g], out_w[g] = jnp.where(here, in_v, in_w[g]), jnp.where(here, out_v, out_w[g])
+        in_wr[g], out_wr[g] = jnp.where(here, in_scaled, in_wr[g]), jnp.where(here, out_scaled, out_wr[g])
+        squares[g] = jnp.where(here, square, squares[g])
+    return jnp.concatenate([(in_w[g] + out_w[g]) * lax.rsqrt(squares[g] + BASIS_EPS) for g in range(4)], axis=0)
 
 
 def factor_kernel(
-    mean, merged, in_basis, out_basis, in_update, out_update, in_error, out_error, in_right, out_right, left
+    mean, merged, in_basis, out_basis, extra, token_grad_in,
+    in_update, out_update, in_error, out_error, in_right, out_right, gain_grad, table_grad, token_grad, left,
 ):
     split = 3 * WIDTH
     left[:, :BLOCK] = nt(in_basis[...], mean[:, :split], precision=HIGH)
     left[:, BLOCK:] = nt(out_basis[...], mean[:, split:], precision=HIGH)
-
-    lane = lax.broadcasted_iota(jnp.int32, (8, 128), 1)
-    row = lax.broadcasted_iota(jnp.int32, (8, 128), 0)
-    is_in = lane < BLOCK
-
-    def half_sums(a):
-        in_sum = jnp.sum(jnp.where(is_in, a, 0.0), axis=1, keepdims=True)
-        out_sum = jnp.sum(jnp.where(is_in, 0.0, a), axis=1, keepdims=True)
-        return jnp.where(is_in, in_sum, out_sum)
-
-    finished = []
-    for c in range(32):
-        column = jnp.broadcast_to(left[c : c + 1, :], (8, 128))
-        if c:
-            for _ in range(2):
-                taken = None
-                for group in finished:
-                    term = group * half_sums(group * column)
-                    taken = term if taken is None else taken + term
-                column = column - jnp.sum(taken, axis=0, keepdims=True)
-        column = column * lax.rsqrt(half_sums(column * column) + BASIS_EPS)
-        if c % 8 == 0:
-            finished.append(jnp.where(row == 0, column, 0.0))
-        else:
-            finished[-1] = jnp.where(row == c % 8, column, finished[-1])
-    ortho = jnp.concatenate(finished, axis=0)
+    ortho = orthonormal_rows(left)
     in_ortho, out_ortho = ortho[:, :BLOCK], ortho[:, BLOCK:]
     right = nn(in_ortho, mean[:, :split], precision=HIGH)
     in_right[...] = right
@@ -525,8 +585,20 @@
     out_update[...] = update
     out_error[...] = merged[:, split:] - update
 
-
-def factors(mean, merged, in_basis, out_basis):
+    share = 1.0 / (N_Y * N_Z * N_MP)
+    buckets = table_grad.shape[1]
+    for head in range(HEADS):
+        for c in range(CHUNKS):
+            width = min(128, buckets - 128 * c)
+            table_grad[head : head + 1, 128 * c : 128 * c + width] = extra[head, c : c + 1, :width] * share
+    for pair in range(HEADS // 2):
+        low, high = extra[2 * pair, 6:7, :], pltpu.roll(extra[2 * pair + 1, 6:7, :], 64, 1)
+        lane = lax.broadcasted_iota(jnp.int32, (1, 128), 1)
+        gain_grad[:, 128 * pair : 128 * (pair + 1)] = jnp.where(lane < 64, low, high) * share
+    token_grad[...] = token_grad_in[...]
+
+
+def factors(buckets, *operands):
     wide = jax.ShapeDtypeStruct((BLOCK, 3 * WIDTH), F32)
     thin = jax.ShapeDtypeStruct((BLOCK, WIDTH), F32)
     return pl.pallas_call(
@@ -535,13 +607,16 @@
             wide, thin, wide, thin,
             jax.ShapeDtypeStruct((32, 3 * WIDTH), F32),
             jax.ShapeDtypeStruct((32, WIDTH), F32),
+            jax.ShapeDtypeStruct((1, WIDTH), F32),
+            jax.ShapeDtypeStruct((HEADS, buckets), F32),
+            jax.ShapeDtypeStruct((ROWS, WIDTH), BF16),
         ),
-        in_specs=[VMEM] * 4,
-        out_specs=(VMEM,) * 6,
+        in_specs=[VMEM] * len(operands),
+        out_specs=(VMEM,) * 9,
         scratch_shapes=[pltpu.VMEM((32, 128), F32)],
         compiler_params=pltpu.CompilerParams(vmem_limit_bytes=32 << 20),
         name="factors",
-    )(mean, merged, in_basis, out_basis)
+    )(*operands)
 
 
 def shards(
@@ -558,24 +633,19 @@
     in_basis,
     out_basis,
 ):
-    devices = lax.axis_size("dp") * lax.axis_size("mp")
-    buckets = bias_table.shape[1]
-    full_in, full_out = gather_weights(in_weight, out_weight)
-    table = jnp.pad(bias_table, ((0, 0), (0, CHUNKS * 128 - buckets)))
-    bias = bias_lookup(table, rel_bucket)
+    tok = tokens.reshape(ROWS, WIDTH)
+    gain = norm_gain.reshape(1, WIDTH)
+    full_in, full_out, bias, normed = gather_weights(in_weight, out_weight, bias_table, rel_bucket, tok, gain)
     token_grad, merged, mean, extra_all = layer(
-        tokens.reshape(ROWS, WIDTH), cotangent.reshape(ROWS, WIDTH), region_ids, rel_bucket, bias,
-        norm_gain.reshape(1, WIDTH), full_in, full_out, in_error[0], out_error[0],
+        cotangent.reshape(ROWS, WIDTH), region_ids, in_error[0], out_error[0], tok, gain, rel_bucket,
+        bias, normed, full_in, full_out,
     )
-    in_update, out_update, in_new, out_new, in_right, out_right = factors(
-        mean, merged, in_basis[0].T, out_basis[0].T
+    in_update, out_update, in_new, out_new, in_right, out_right, gain_grad, table_grad, token_grad = factors(
+        bias_table.shape[1], mean, merged, in_basis[0].T, out_basis[0].T, extra_all, token_grad
     )
-    extra_all = extra_all * (1.0 / devices)
-    gain_grad = extra_all[:, 6, :64].reshape(WIDTH)
-    table_grad = extra_all[:, :CHUNKS, :].reshape(HEADS, CHUNKS * 128)[:, :buckets]
     return (
         token_grad.reshape(tokens.shape),
-        gain_grad,
+        gain_grad.reshape(WIDTH),
         table_grad,
         in_update,
         out_update,

time: 106 us -> 92.3 us (0.87)
  Pallas kernels: 99.1 us -> 91.4 us
  local copies, waits for them, and re-layouts: 5.47 us -> 0.01 us
    unnamed x27 -> x4, local copies, waits for them, and re-layouts: 4.04 us -> 0.01 us
    pallas_call x1 -> x0, Pallas kernels: 3.43 us -> none  [bias_lookup(): pl.pallas_call(bias_kernel, out_shape=jax.ShapeDtypeStruct((HEADS, SPAN,...]
    pallas_call x1, Pallas kernels: 10.9 us -> 8.42 us  [factors(): pl.pallas_call(factor_kernel, out_shape=(wide, thin, wide, thin, jax.Shap...]
    pallas_call x1, Pallas kernels: 65.4 us -> 64 us  [layer(): pl.pallas_call(layer_kernel, out_shape=(jax.ShapeDtypeStruct((ROWS, WIDTH...]
where the time goes in v3:
time: 92.3 us; the launch traced here: 92.1 us
  Pallas kernels  91.4 us (99%)
    pallas_call x1, Pallas kernels, layer(): pl.pallas_call(layer_kernel, out_shape=(jax.ShapeDtypeStruct((ROWS, WIDTH...  64 us
    pallas_call x1, Pallas kernels, gather_weights(): pl.pallas_call(gather_kernel, out_shape=(jax.ShapeDtypeStruct((WIDTH, 3 *...  19 us
    pallas_call x1, Pallas kernels, factors(): pl.pallas_call(factor_kernel, out_shape=(wide, thin, wide, thin, jax.Shap...  8.42 us

profile of v3, /device:TPU:1, one launch (start us, length us, event | category | flops | bytes accessed | tf_op | source)
XLA Modules:
  0.0 92.1 jit_solution(7380325643862964350)
XLA Ops:
  0.6 19.0 %gather_weights.1 = (bf16[512,1536]{1,0:T(8,128)(2,1)S(1)}, bf16[512,512]{1,0:T(8,128)(2,1)S(1)}, f32[8,144,144]{2,1,0:T(8,128)S(1)}, bf16[288,512]{1,0:T(8,128)(2,1)S(1)}) custom-call(bf16[64,1536]{1,0:T(8,128)(2,1)} %in_ref.1, bf16[64,512]{1,0:T(8,128)(2,1)} %out_ref.1, f32[8,759]{1,0:T(8,128)} %table_hbm.1, s32[144,144]{1,0:T(8,128)} %bucket_hbm.3, ...), custom_call_target="tpu_custom_call" | custom-call | tf_op jit(solution)/shard_map/gather_weights/pallas_call | solution.py:156
  19.7 0.0 copy-start
  19.7 0.0 copy-start.1
  19.7 64.0 %layer.1 = (bf16[288,512]{1,0:T(8,128)(2,1)S(1)}, f32[64,2048]{1,0:T(8,128)S(1)}, f32[64,2048]{1,0:T(8,128)S(1)}, f32[8,8,128]{2,1,0:T(8,128)S(1)}) custom-call(bf16[288,512]{1,0:T(8,128)(2,1)} %bitcast.26, s32[2,144]{1,0:T(2,128)} %region_hbm.1, f32[64,1536]{1,0:T(8,128)} %bitcast.25, f32[64,512]{1,0:T(8,128)} %bitcast.27, bf16[288,512]{1,0:T(8,128)(2,1)} %bitcast.24, ...), custom_call_target="tpu_custom_call" | custom-call | tf_op jit(solution)/shard_map/layer/pallas_call | solution.py:480
  83.7 0.0 copy-done
  83.7 0.0 copy-done.1
  83.7 8.4 %factors.1 = (f32[64,1536]{1,0:T(8,128)}, f32[64,512]{1,0:T(8,128)}, f32[64,1536]{1,0:T(8,128)}, f32[64,512]{1,0:T(8,128)}, f32[32,1536]{1,0:T(8,128)}, /*index=...) custom-call(f32[64,2048]{1,0:T(8,128)S(1)} %get-tuple-element.30.mean, ...), custom_call_target="tpu_custom_call" | custom-call | tf_op jit(solution)/shard_map/factors/pallas_call | solution.py:604
Async XLA Ops:
  19.7 64.0 %copy-start = (f32[1,1536,32]{1,2,0:T(8,128)S(1)}, f32[1,1536,32]{1,2,0:T(8,128)}, u32[]{:S(2)}) copy-start(f32[1,1536,32]{1,2,0:T(8,128)} %param.22) | copy-start | bytes 589828
  19.7 64.0 %copy-start.1 = (f32[1,512,32]{1,2,0:T(8,128)S(1)}, f32[1,512,32]{1,2,0:T(8,128)}, u32[]{:S(2)}) copy-start(f32[1,512,32]{1,2,0:T(8,128)} %param.23) | copy-start | bytes 196612

commit v4 on v3

--- a/solution.py
+++ b/solution.py
@@ -36,7 +36,7 @@
 
 def gather_kernel(
     in_ref, out_ref, table_hbm, bucket_hbm, tok_hbm, gain_hbm,
-    full_in, full_out, bias_ref, normed_ref,
+    full_in, full_out, bias_ref, normed_ref, flipped_ref,
     table_ref, bucket_ref, tok_ref, gain_ref, index, table, send, recv, rsend, rrecv, fsend, frecv, local,
 ):
     mp = lax.axis_index("mp")
@@ -132,7 +132,9 @@
     wide = tok_ref[...].astype(F32)
     centered = wide - jnp.mean(wide, axis=-1, keepdims=True)
     inv_sigma = lax.rsqrt(jnp.mean(centered * centered, axis=-1, keepdims=True) + NORM_EPS)
-    normed_ref[...] = (centered * inv_sigma * gain_ref[...]).astype(BF16)
+    rounded = (centered * inv_sigma * gain_ref[...]).astype(BF16)
+    normed_ref[...] = rounded
+    flipped_ref[...] = rounded.T
     for k in range(2):
         for way in range(2):
             first[way, k, 1 - way].wait_recv()
@@ -160,9 +162,10 @@
             jax.ShapeDtypeStruct((WIDTH, WIDTH), BF16),
             jax.ShapeDtypeStruct((HEADS, SPAN, SPAN), F32),
             jax.ShapeDtypeStruct((ROWS, WIDTH), BF16),
+            jax.ShapeDtypeStruct((WIDTH, ROWS), BF16),
         ),
         in_specs=[HBM] * len(operands),
-        out_specs=(VMEM,) * 4,
+        out_specs=(VMEM,) * 5,
         scratch_shapes=[pltpu.VMEM(a.shape, a.dtype) for a in operands[2:]]
         + [pltpu.VMEM((SPAN, 256), jnp.int32), pltpu.VMEM((HEADS, CHUNKS * 128), F32)]
         + dma(2, 2, 2) + dma(2, 2) + dma(4, 2, 2)
@@ -172,20 +175,60 @@
     )(*(pltpu.with_memory_space_constraint(a, pltpu.HBM) for a in operands))
 
 
+def orthonormal_rows(left, halfway):
+    lane = lax.broadcasted_iota(jnp.int32, (8, 128), 1)
+    row = lax.broadcasted_iota(jnp.int32, (8, 128), 0)
+    is_in = lane < BLOCK
+    zero = jnp.zeros((8, 128), F32)
+
+    def lane_sum(a):
+        return jnp.sum(a, axis=1, keepdims=True)
+
+    columns = [left[8 * g : 8 * g + 8, :] for g in range(4)]
+    in_columns = [jnp.where(is_in, v, 0.0) for v in columns]
+    out_columns = [jnp.where(is_in, 0.0, v) for v in columns]
+    taken = [zero] * 4
+    in_w, out_w, in_wr, out_wr, squares = ([zero] * 4 for _ in range(5))
+    for c in range(32):
+        g, at = c // 8, c % 8
+        if c == 16:
+            halfway()
+        here = row == at
+        vector = jnp.broadcast_to((columns[g] - taken[g])[at : at + 1, :], (8, 128))
+        if c:
+            total = None
+            for k in range(g + 1):
+                term = in_wr[k] * lane_sum(in_w[k] * vector) + out_wr[k] * lane_sum(out_w[k] * vector)
+                total = term if total is None else total + term
+            vector = vector - jnp.sum(total, axis=0, keepdims=True)
+        in_v, out_v = jnp.where(is_in, vector, 0.0), jnp.where(is_in, 0.0, vector)
+        square = jnp.where(is_in, lane_sum(in_v * in_v), lane_sum(out_v * out_v))
+        share = 1.0 / (square + BASIS_EPS)
+        in_scaled, out_scaled = in_v * share, out_v * share
+        for k in range(g, 4):
+            taken[k] = (
+                taken[k] + in_scaled * lane_sum(in_columns[k] * vector) + out_scaled * lane_sum(out_columns[k] * vector)
+            )
+        in_w[g], out_w[g] = jnp.where(here, in_v, in_w[g]), jnp.where(here, out_v, out_w[g])
+        in_wr[g], out_wr[g] = jnp.where(here, in_scaled, in_wr[g]), jnp.where(here, out_scaled, out_wr[g])
+        squares[g] = jnp.where(here, square, squares[g])
+    return jnp.concatenate([(in_w[g] + out_w[g]) * lax.rsqrt(squares[g] + BASIS_EPS) for g in range(4)], axis=0)
+
+
 def layer_kernel(
-    cot_hbm, region_hbm, in_error_hbm, out_error_hbm, tok_hbm, gain_hbm, bucket_hbm,
-    bias_ref, normed, win_ref, wout_ref,
-    tokgrad_ref, merged, mean, extra_all,
-    cot_ref, region_ref, in_error, out_error, tok_ref, gain_ref, bucket_ref, staging,
+    cot_hbm, region_hbm, in_error_hbm, out_error_hbm, tok_hbm, gain_hbm, bucket_hbm, in_basis_hbm, out_basis_hbm,
+    bias_ref, normed, flipped, win_ref, wout_ref,
+    tokgrad_ref, merged, mean, extra_all, ortho,
+    cot_ref, region_ref, in_error, out_error, tok_ref, gain_ref, bucket_ref, in_basis, out_basis, staging,
     proj, mixgrad, mixed, packed, x_hat, score_high, score_low,
-    prod, near, mine, far,
+    prod, near, mine, far, out_prod, out_near, out_mine, out_far,
     err_y, err_slab, err_z, err_full,
-    sum_src, sum_y, sum_slab, sum_z, sum_full,
-    ex, ex_near, ex_mine, ex_far, ex_part, ex_y, ex_z,
-    s_near, r_near, s_far, r_far,
+    sum_src, out_src, sum_own, sum_y, sum_slab, sum_z, sum_full,
+    ex, ex_near, ex_mine, ex_far, ex_part, ex_y, ex_z, left_all,
+    s_near, r_near, s_far, r_far, s_fo, r_fo,
     s_ey, r_ey, s_ez, r_ez, s_ezz, r_ezz, s_eyy, r_eyy,
     s_ty, r_ty, s_tz, r_tz, s_tzz, r_tzz, s_tyy, r_tyy,
-    s_xn, r_xn, s_xf, r_xf, s_xy, r_xy, s_xz, r_xz, s_xx, r_xx, s_xs, r_xs,
+    s_xn, r_xn, s_xf, r_xf, s_xy, r_xy, s_xz, r_xz, s_xx, r_xx, s_xs, r_xs, s_l, r_l,
 ):
     dp, mp = lax.axis_index("dp"), lax.axis_index("mp")
     z, y, x, core = dp // N_Y, dp % N_Y, mp // 2, mp % 2
@@ -227,6 +270,7 @@
             (
                 (cot_hbm, cot_ref), (region_hbm, region_ref), (in_error_hbm, in_error), (out_error_hbm, out_error),
                 (tok_hbm, tok_ref), (gain_hbm, gain_ref), (bucket_hbm, bucket_ref),
+                (in_basis_hbm, in_basis), (out_basis_hbm, out_basis),
             )
         )
     ]
@@ -247,8 +291,7 @@
         square = jnp.broadcast_to(region_ref[w : w + 1, :].astype(F32), (SPAN, SPAN))
         allowed.append(square == square.T)
 
-    @pl.loop(0, HEADS // 2)
-    def _(pair):
+    def heads(pair):
         at = [pl.ds(pl.multiple_of(k * WIDTH + pair * 128, 128), 128) for k in range(3)]
         grads = [[], []]
         for w in range(WIN):
@@ -275,48 +318,64 @@
             joined = [jnp.where(first_half, a, b).astype(BF16) for a, b in zip(*parts)]
             for k in range(3):
                 packed[rows, at[k]] = joined[k]
-            mixed[rows, at[0]] = joined[3]
+            mixed[rows, :] = joined[3]
         for t in range(2):
             total = grads[t][0] + grads[t][1]
             high = total.astype(BF16).astype(F32)
             score_high[2 * pair + t] = high
             score_low[2 * pair + t] = total - high
-
-    pl.semaphore_wait(barrier, len(peers))
+        return at
+
+    order = (2, 1, 3, 0)
+    near_in, near_out, far_in, far_out = {}, {}, {}, {}
+
+    def send_near(i, at):
+        columns = jnp.concatenate([packed[:, at[k]] for k in range(3)], axis=1)
+        terms = nn(flipped[...], columns).astype(BF16)
+        for m in range(N_MP):
+            prod[i, m // 2, m % 2] = terms[m * BLOCK : (m + 1) * BLOCK]
+        out_terms = tn(mixed[...], cot_ref[...]).astype(BF16)
+        for c in range(2):
+            out_prod[i, c] = out_terms[c * BLOCK : (c + 1) * BLOCK]
+        near_in[i] = remote(prod.at[i, :, 1 - core], near.at[i], s_near.at[i, 0], r_near.at[i, 0], sibling)
+        near_out[i] = remote(out_prod.at[i, 1 - core], out_near.at[i], s_near.at[i, 1], r_near.at[i, 1], sibling)
+
+    def send_far(i):
+        near_in[i].wait_recv()
+        for s in four:
+            chip = (x + s) % N_X
+            mine[i, s] = (prod[i, chip, core].astype(F32) + near[i, chip].astype(F32)).astype(BF16)
+            pair = pair_of(i)
+            far_in[i, s] = remote(mine.at[i, s], far.at[pair, s], s_far.at[i, s], r_far.at[pair, s], x_peer(s))
+        near_out[i].wait_recv()
+        s = order[i]
+        if s:
+            out_mine[s] = (out_prod[i, core].astype(F32) + out_near[i].astype(F32)).astype(BF16)
+            far_out[s] = remote(out_mine.at[s], out_far.at[s], s_fo.at[s], r_fo.at[s], x_peer(s))
+
+    def pair_of(i):
+        return (x + order[i]) % N_X
 
     e_y = []
-    for s in four:
-        rows = slab_rows((y + s) % N_Y)
-        e_y.append(remote(in_error.at[rows], err_y.at[s, :, pl.ds(0, split)], s_ey.at[s, 0], r_ey.at[s, 0], y_peer(s)))
-        e_y.append(
-            remote(out_error.at[rows], err_y.at[s, :, pl.ds(split, WIDTH)], s_ey.at[s, 1], r_ey.at[s, 1], y_peer(s))
-        )
-
-    first = {}
-    for s in (2, 1, 3, 0):
-        cols = pl.ds(pl.multiple_of(((x + s) % N_X) * 128, 128), 128)
-        prod[s, :, :split] = tn(normed[:, cols], packed[...]).astype(BF16)
-        prod[s, :, split:] = tn(mixed[:, cols], cot_ref[...]).astype(BF16)
-        other = pl.ds(pl.multiple_of((1 - core) * BLOCK, BLOCK), BLOCK)
-        first[s] = remote(prod.at[s, other], near.at[s], s_near.at[s], r_near.at[s], sibling)
-    own = pl.ds(pl.multiple_of(core * BLOCK, BLOCK), BLOCK)
-    second = {}
-
-    def send_second(s, c):
-        rows = slab_rows((y + c) % N_Y)
-        second[s, c] = remote(mine.at[s, rows], far.at[s, rows], s_far.at[s, c], r_far.at[s, c], x_peer(s))
-
-    for s in four:
-        first[s].wait_recv()
-        mine[s] = (prod[s, own].astype(F32) + near[s].astype(F32)).astype(BF16)
-        if s == 2:
-            for c in (2, 1, 3, 0):
-                send_second(s, c)
-    for c in (2, 1, 3, 0):
-        send_second(1, c)
-        send_second(3, c)
-    first[0].wait_recv()
-    merged[...] = prod[0, own].astype(F32) + near[0].astype(F32)
+
+    def error_over_y():
+        for s in four:
+            rows = slab_rows((y + s) % N_Y)
+            e_y.append(remote(in_error.at[rows], err_y.at[s, :, pl.ds(0, split)], s_ey.at[s, 0], r_ey.at[s, 0], y_peer(s)))
+            e_y.append(
+                remote(out_error.at[rows], err_y.at[s, :, pl.ds(split, WIDTH)], s_ey.at[s, 1], r_ey.at[s, 1], y_peer(s))
+            )
+
+    for i in range(4):
+        at = heads(pair_of(i))
+        if i == 0:
+            pl.semaphore_wait(barrier, len(peers))
+        send_near(i, at)
+        if i == 0:
+            error_over_y()
+        if i:
+            send_far(i - 1)
+
 
     for copy in e_y:
         copy.wait_recv()
@@ -343,12 +402,14 @@
     )
     tokgrad_ref[...] = (cot_ref[...].astype(F32) + delta).astype(BF16)
 
+    send_far(3)
+
     chunk_row = lax.broadcasted_iota(jnp.int32, (8, SPAN), 0)
     within = lax.broadcasted_iota(jnp.int32, (128, SPAN), 0)
 
     def add_rows(block, total):
-        for k in range(8):
-            i = block * 8 + k
+        for k in range(16):
+            i = block * 16 + k
             bucket = bucket_ref[pl.ds(i, 1), :]
             chunk_is = jnp.broadcast_to(bucket >> 7, (8, SPAN)) == chunk_row
             one_hot = jnp.where(jnp.broadcast_to(bucket & 127, (128, SPAN)) == within, 1.0, 0.0).astype(BF16)
@@ -363,7 +424,7 @@
             total = total + nt(picked, one_hot)
         return total
 
-    total = lax.fori_loop(0, SPAN // 8, add_rows, jnp.zeros((128, 128), F32))
+    total = lax.fori_loop(0, SPAN // 16, add_rows, jnp.zeros((128, 128), F32))
     table_term = total[:64] + total[64:]
     for head in range(HEADS):
         ex[head // 2, head % 2] = table_term[8 * head : 8 * head + 8]
@@ -375,6 +436,37 @@
         s: remote(ex.at[(x + s) % N_X, 1 - core], ex_near.at[s], s_xn.at[s], r_xn.at[s], sibling) for s in (2, 1, 3, 0)
     }
 
+    t_y = {}
+    totals = []
+
+    def send_y(j, total, src, width):
+        src[...] = total.astype(BF16)
+        for s in four:
+            rows = slab_rows((y + s) % N_Y)
+            t_y[j, s] = remote(
+                src.at[rows], sum_y.at[j, s, :, pl.ds(0, width)], s_ty.at[j, s], r_ty.at[j, s], y_peer(s)
+            )
+
+    for i in range(4):
+        total = prod[i, x, core].astype(F32) + near[i, x].astype(F32)
+        for s in (1, 3, 2):
+            far_in[i, s].wait_recv()
+            total = total + far[pair_of(i), s].astype(F32)
+        total = total * (1.0 / N_MP)
+        for k in range(3):
+            cols = pl.ds(pl.multiple_of(k * WIDTH + pair_of(i) * 128, 128), 128)
+            merged[:, cols] = total[:, 128 * k : 128 * (k + 1)] + in_error[:, cols]
+        send_y(i, total, sum_src.at[i], 384)
+        sum_own[i, :, :384] = total
+    total = out_prod[3, core].astype(F32) + out_near[3].astype(F32)
+    for s in (2, 1, 3):
+        far_out[s].wait_recv()
+        total = total + out_far[s].astype(F32)
+    total = total * (1.0 / N_MP)
+    merged[:, split:] = total + out_error[...]
+    send_y(4, total, out_src, WIDTH)
+    sum_own[4] = total
+
     piece = err_slab[z]
     for s in near_first:
         e_z[s].wait_recv()
@@ -383,29 +475,20 @@
     here = err_full.at[y, z]
     e_zz = {s: remote(here, here, s_ezz.at[s], r_ezz.at[s], z_peer(s)) for s in z_steps}
 
-    t_y = {}
     x_far = {}
-    for c in (2, 1, 3, 0):
-        rows = slab_rows((y + c) % N_Y)
+    for s in four:
+        x_near[s].wait_recv()
+        ex_mine[s] = ex[(x + s) % N_X, core] + ex_near[s]
+        x_far[s] = remote(ex_mine.at[s], ex_far.at[s], s_xf.at[s], r_xf.at[s], x_peer(s))
+
+    for j in range(5):
+        total = sum_own[j, slab_rows(y), :]
         for s in (1, 3, 2):
-            second[s, c].wait_recv()
-        total = merged[rows, :] + far[1, rows].astype(F32) + far[3, rows].astype(F32) + far[2, rows].astype(F32)
-        total = total * (1.0 / N_MP)
-        merged[rows, :split] = total[:, :split] + in_error[rows, :]
-        merged[rows, split:] = total[:, split:] + out_error[rows, :]
-        if c:
-            sum_src[rows, :] = total.astype(BF16)
-            t_y[c] = remote(sum_src.at[rows], sum_y.at[c], s_ty.at[c], r_ty.at[c], y_peer(c))
-        if c == 2:
-            for s in four:
-                x_near[s].wait_recv()
-                ex_mine[s] = ex[(x + s) % N_X, core] + ex_near[s]
-                x_far[s] = remote(ex_mine.at[s], ex_far.at[s], s_xf.at[s], r_xf.at[s], x_peer(s))
-    for s in four:
-        t_y[s].wait_recv()
-        total = total + sum_y[s].astype(F32)
-    for k in range(N_Z):
-        sum_slab[k] = total[:, 128 * k : 128 * (k + 1)]
+            t_y[j, s].wait_recv()
+            total = total + sum_y[j, s].astype(F32)
+        for k in range(3 if j < 4 else 4):
+            piece_at = 4 * k + pair_of(j) if j < 4 else 12 + k
+            sum_slab[piece_at] = total[:, 128 * k : 128 * (k + 1)]
     rounded = sum_slab[...].astype(BF16)
     sum_send = sum_full.at[N_Y]
     sum_full[N_Y] = rounded
@@ -419,11 +502,6 @@
     ex_part[0] = part
     x_y = {s: remote(ex_part.at[0], ex_y.at[s], s_xy.at[s], r_xy.at[s], y_peer(s)) for s in four}
 
-    for s in near_first:
-        e_zz[s].wait_recv()
-    here = err_full.at[y]
-    e_yy = {s: remote(here, here, s_eyy.at[s], r_eyy.at[s], y_peer(s)) for s in four}
-
     piece = sum_slab[z]
     for s in near_first:
         t_z[s].wait_recv()
@@ -432,14 +510,31 @@
     here = sum_full.at[y, z]
     t_zz = {s: remote(here, here, s_tzz.at[s], r_tzz.at[s], z_peer(s)) for s in z_steps}
 
+    for s in near_first:
+        e_zz[s].wait_recv()
+    here = err_full.at[y]
+    e_yy = {s: remote(here, here, s_eyy.at[s], r_eyy.at[s], y_peer(s)) for s in four}
+
     for s in four:
         x_y[s].wait_recv()
         part = part + ex_y[s]
     ex_part[1] = part
     x_z = {s: remote(ex_part.at[1], ex_z.at[s], s_xz.at[s], r_xz.at[s], z_peer(s)) for s in z_steps}
 
+    def finish(slab):
+        for k in range(N_Z):
+            mean[slab_rows(slab), 128 * k : 128 * (k + 1)] = err_full[slab, k] + sum_full[slab, k].astype(F32)
+
     for s in near_first:
         t_zz[s].wait_recv()
+    finish(y)
+
+    slab = mean[slab_rows(y), :]
+    in_left = nt(slab[:, :split], in_basis[...], precision=HIGH)
+    out_left = nt(slab[:, split:], out_basis[...], precision=HIGH)
+    left_all[y] = jnp.concatenate([in_left, out_left, jnp.zeros((16, 64), F32)], axis=1)
+    here = left_all.at[y]
+    left_y = {s: remote(here, here, s_l.at[s], r_l.at[s], y_peer(s)) for s in four}
     here = sum_full.at[y]
     t_yy = {s: remote(here, here, s_tyy.at[s], r_tyy.at[s], y_peer(s)) for s in four}
 
@@ -451,15 +546,18 @@
     x_x = {s: remote(here, here, s_xx.at[s], r_xx.at[s], x_peer(s)) for s in four}
     x_s = [remote(here, here, s_xs.at[0], r_xs.at[0], sibling)]
 
-    def finish(slab):
-        for k in range(N_Z):
-            mean[slab_rows(slab), 128 * k : 128 * (k + 1)] = err_full[slab, k] + sum_full[slab, k].astype(F32)
-
-    finish(y)
     for s in (1, 3, 2):
-        x_x[s].wait_recv()
-        here = extra_all.at[2 * ((x + N_X - s) % N_X) + core]
-        x_s.append(remote(here, here, s_xs.at[s], r_xs.at[s], sibling))
+        left_y[s].wait_recv()
+    flipped_left = left_all[...].reshape(BLOCK, 128).T
+
+    def halfway():
+        for s in (1, 3, 2):
+            x_x[s].wait_recv()
+            here = extra_all.at[2 * ((x + N_X - s) % N_X) + core]
+            x_s.append(remote(here, here, s_xs.at[s], r_xs.at[s], sibling))
+
+    ortho[...] = orthonormal_rows(jnp.concatenate([flipped_left[:32], flipped_left[32:64]], axis=1), halfway)
+
     for s in (1, 3, 2):
         e_yy[s].wait_recv()
         t_yy[s].wait_recv()
@@ -484,29 +582,36 @@
             jax.ShapeDtypeStruct((BLOCK, COLS), F32),
             jax.ShapeDtypeStruct((BLOCK, COLS), F32),
             jax.ShapeDtypeStruct((N_MP, 8, 128), F32),
+            jax.ShapeDtypeStruct((32, 2 * BLOCK), F32),
         ),
-        in_specs=[HBM] * 7 + [VMEM] * 4,
-        out_specs=(VMEM,) * 4,
-        scratch_shapes=[pltpu.VMEM(a.shape, a.dtype) for a in operands[:7]]
-        + [pltpu.SemaphoreType.DMA((7,))]
+        in_specs=[HBM] * 9 + [VMEM] * 5,
+        out_specs=(VMEM,) * 5,
+        scratch_shapes=[pltpu.VMEM(a.shape, a.dtype) for a in operands[:9]]
+        + [pltpu.SemaphoreType.DMA((9,))]
         + [
             vmem(ROWS, 3 * WIDTH, dtype=BF16),
             vmem(ROWS, WIDTH, dtype=BF16),
-            vmem(ROWS, WIDTH, dtype=BF16),
+            vmem(ROWS, 128, dtype=BF16),
             vmem(ROWS, 3 * WIDTH, dtype=BF16),
             vmem(ROWS, WIDTH),
             vmem(HEADS, SPAN, SPAN),
             vmem(HEADS, SPAN, SPAN),
-            vmem(N_X, 2 * BLOCK, COLS, dtype=BF16),
-            vmem(N_X, BLOCK, COLS, dtype=BF16),
-            vmem(N_X, BLOCK, COLS, dtype=BF16),
-            vmem(N_X, BLOCK, COLS, dtype=BF16),
+            vmem(4, N_X, 2, BLOCK, 384, dtype=BF16),
+            vmem(4, N_X, BLOCK, 384, dtype=BF16),
+            vmem(4, N_X, BLOCK, 384, dtype=BF16),
+            vmem(4, N_X, BLOCK, 384, dtype=BF16),
+            vmem(4, 2, BLOCK, WIDTH, dtype=BF16),
+            vmem(4, BLOCK, WIDTH, dtype=BF16),
+            vmem(N_X, BLOCK, WIDTH, dtype=BF16),
+            vmem(N_X, BLOCK, WIDTH, dtype=BF16),
             vmem(N_Y, 16, COLS),
             vmem(N_Z, 16, 128),
             vmem(N_Z, 16, 128),
             vmem(N_Y, N_Z, 16, 128),
-            vmem(BLOCK, COLS, dtype=BF16),
-            vmem(N_Y, 16, COLS, dtype=BF16),
+            vmem(4, BLOCK, 384, dtype=BF16),
+            vmem(BLOCK, WIDTH, dtype=BF16),
+            vmem(5, BLOCK, WIDTH),
+            vmem(5, N_Y, 16, WIDTH, dtype=BF16),
             vmem(N_Z, 16, 128),
             vmem(N_Z, 16, 128, dtype=BF16),
             vmem(N_Y + 1, N_Z, 16, 128, dtype=BF16),
@@ -517,62 +622,22 @@
             vmem(2, 8, 128),
             vmem(N_Y, 8, 128),
             vmem(N_Z, 8, 128),
+            vmem(N_Y, 16, 128),
         ]
-        + dma(4) + dma(4, 4)
+        + dma(4, 2) + dma(4, 4) + dma(4)
         + dma(4, 2) + dma(N_Z) + dma(N_Z) + dma(4)
-        + dma(4) + dma(N_Z) + dma(N_Z) + dma(4)
-        + dma(4) + dma(4) + dma(4) + dma(N_Z) + dma(4) + dma(4),
+        + dma(5, 4) + dma(N_Z) + dma(N_Z) + dma(4)
+        + dma(4) + dma(4) + dma(4) + dma(N_Z) + dma(4) + dma(4) + dma(4),
         compiler_params=pltpu.CompilerParams(collective_id=1, has_side_effects=True, vmem_limit_bytes=48 << 20),
         name="layer",
-    )(*(pltpu.with_memory_space_constraint(a, pltpu.HBM) for a in operands[:7]), *operands[7:])
-
-
-def orthonormal_rows(left):
-    lane = lax.broadcasted_iota(jnp.int32, (8, 128), 1)
-    row = lax.broadcasted_iota(jnp.int32, (8, 128), 0)
-    is_in = lane < BLOCK
-    zero = jnp.zeros((8, 128), F32)
-
-    def lane_sum(a):
-        return jnp.sum(a, axis=1, keepdims=True)
-
-    columns = [left[8 * g : 8 * g + 8, :] for g in range(4)]
-    in_columns = [jnp.where(is_in, v, 0.0) for v in columns]
-    out_columns = [jnp.where(is_in, 0.0, v) for v in columns]
-    taken = [zero] * 4
-    in_w, out_w, in_wr, out_wr, squares = ([zero] * 4 for _ in range(5))
-    for c in range(32):
-        g, at = c // 8, c % 8
-        here = row == at
-        vector = jnp.broadcast_to((columns[g] - taken[g])[at : at + 1, :], (8, 128))
-        if c:
-            total = None
-            for k in range(g + 1):
-                term = in_wr[k] * lane_sum(in_w[k] * vector) + out_wr[k] * lane_sum(out_w[k] * vector)
-                total = term if total is None else total + term
-            vector = vector - jnp.sum(total, axis=0, keepdims=True)
-        in_v, out_v = jnp.where(is_in, vector, 0.0), jnp.where(is_in, 0.0, vector)
-        square = jnp.where(is_in, lane_sum(in_v * in_v), lane_sum(out_v * out_v))
-        share = 1.0 / (square + BASIS_EPS)
-        in_scaled, out_scaled = in_v * share, out_v * share
-        for k in range(g, 4):
-            taken[k] = (
-                taken[k] + in_scaled * lane_sum(in_columns[k] * vector) + out_scaled * lane_sum(out_columns[k] * vector)
-            )
-        in_w[g], out_w[g] = jnp.where(here, in_v, in_w[g]), jnp.where(here, out_v, out_w[g])
-        in_wr[g], out_wr[g] = jnp.where(here, in_scaled, in_wr[g]), jnp.where(here, out_scaled, out_wr[g])
-        squares[g] = jnp.where(here, square, squares[g])
-    return jnp.concatenate([(in_w[g] + out_w[g]) * lax.rsqrt(squares[g] + BASIS_EPS) for g in range(4)], axis=0)
+    )(*(pltpu.with_memory_space_constraint(a, pltpu.HBM) for a in operands[:9]), *operands[9:])
 
 
 def factor_kernel(
-    mean, merged, in_basis, out_basis, extra, token_grad_in,
-    in_update, out_update, in_error, out_error, in_right, out_right, gain_grad, table_grad, token_grad, left,
+    mean, merged, ortho, extra, token_grad_in,
+    in_update, out_update, in_error, out_error, in_right, out_right, gain_grad, table_grad, token_grad,
 ):
     split = 3 * WIDTH
-    left[:, :BLOCK] = nt(in_basis[...], mean[:, :split], precision=HIGH)
-    left[:, BLOCK:] = nt(out_basis[...], mean[:, split:], precision=HIGH)
-    ortho = orthonormal_rows(left)
     in_ortho, out_ortho = ortho[:, :BLOCK], ortho[:, BLOCK:]
     right = nn(in_ortho, mean[:, :split], precision=HIGH)
     in_right[...] = right
@@ -613,7 +678,6 @@
         ),
         in_specs=[VMEM] * len(operands),
         out_specs=(VMEM,) * 9,
-        scratch_shapes=[pltpu.VMEM((32, 128), F32)],
         compiler_params=pltpu.CompilerParams(vmem_limit_bytes=32 << 20),
         name="factors",
     )(*operands)
@@ -635,13 +699,14 @@
 ):
     tok = tokens.reshape(ROWS, WIDTH)
     gain = norm_gain.reshape(1, WIDTH)
-    full_in, full_out, bias, normed = gather_weights(in_weight, out_weight, bias_table, rel_bucket, tok, gain)
-    token_grad, merged, mean, extra_all = layer(
+    full_in, full_out, bias, normed, flipped = gather_weights(in_weight, out_weight, bias_table, rel_bucket, tok, gain)
+    token_grad, merged, mean, extra_all, ortho = layer(
         cotangent.reshape(ROWS, WIDTH), region_ids, in_error[0], out_error[0], tok, gain, rel_bucket,
-        bias, normed, full_in, full_out,
+        in_basis[0].T, out_basis[0].T,
+        bias, normed, flipped, full_in, full_out,
     )
     in_update, out_update, in_new, out_new, in_right, out_right, gain_grad, table_grad, token_grad = factors(
-        bias_table.shape[1], mean, merged, in_basis[0].T, out_basis[0].T, extra_all, token_grad
+        bias_table.shape[1], mean, merged, ortho, extra_all, token_grad
     )
     return (
         token_grad.reshape(tokens.shape),

time: 92.3 us -> 85.1 us (0.922)
  Pallas kernels: 91.4 us -> 84.2 us
    pallas_call x1, Pallas kernels: 8.42 us -> 1.84 us  [factors(): pl.pallas_call(factor_kernel, out_shape=(wide, thin, wide, thin, jax.Shap...]
where the time goes in v4:
time: 85.1 us; the launch traced here: 84.9 us
  Pallas kernels  84.2 us (99%)
    pallas_call x1, Pallas kernels, layer(): pl.pallas_call(layer_kernel, out_shape=(jax.ShapeDtypeStruct((ROWS, WIDTH...  63.3 us
    pallas_call x1, Pallas kernels, gather_weights(): pl.pallas_call(gather_kernel, out_shape=(jax.ShapeDtypeStruct((WIDTH, 3 *...  19 us
    pallas_call x1, Pallas kernels, factors(): pl.pallas_call(factor_kernel, out_shape=(wide, thin, wide, thin, jax.Shap...  1.84 us

profile of v4, /device:TPU:1, one launch (start us, length us, event | category | flops | bytes accessed | tf_op | source)
XLA Modules:
  0.0 84.9 jit_solution(11889870628719156585)
XLA Ops:
  0.6 19.0 %gather_weights.1 = (bf16[512,1536]{1,0:T(8,128)(2,1)S(1)}, bf16[512,512]{1,0:T(8,128)(2,1)S(1)}, f32[8,144,144]{2,1,0:T(8,128)S(1)}, bf16[288,512]{1,0:T(8,128)(2,1)S(1)}, bf16[512,288]{1,0:T(8,128)(2,1)S(1)}) custom-call(bf16[64,1536]{1,0:T(8,128)(2,1)} %in_ref.1, bf16[64,512]{1,0:T(8,128)(2,1)} %out_ref.1, f32[8,759]{1,0:T(8,128)} %table_hbm.1, ...), custom_call_target="tpu_custom_call" | custom-call | tf_op jit(solution)/shard_map/gather_weights/pallas_call | solution.py:158
  19.7 63.3 %layer.1 = (bf16[288,512]{1,0:T(8,128)(2,1)S(1)}, f32[64,2048]{1,0:T(8,128)S(1)}, f32[64,2048]{1,0:T(8,128)S(1)}, f32[8,8,128]{2,1,0:T(8,128)S(1)}, f32[32,128]{1,0:T(8,128)S(1)}) custom-call(bf16[288,512]{1,0:T(8,128)(2,1)} %bitcast.24, s32[2,144]{1,0:T(2,128)} %region_hbm.1, f32[64,1536]{1,0:T(8,128)} %bitcast.23, f32[64,512]{1,0:T(8,128)} %bitcast.26, ...), custom_call_target="tpu_custom_call" | custom-call | tf_op jit(solution)/shard_map/layer/pallas_call | solution.py:578
  83.0 1.8 %factors.1 = (f32[64,1536]{1,0:T(8,128)}, f32[64,512]{1,0:T(8,128)}, f32[64,1536]{1,0:T(8,128)}, f32[64,512]{1,0:T(8,128)}, f32[32,1536]{1,0:T(8,128)}, /*index=...) custom-call(f32[64,2048]{1,0:T(8,128)S(1)} %get-tuple-element.33.mean, ...), custom_call_target="tpu_custom_call" | custom-call | tf_op jit(solution)/shard_map/factors/pallas_call | solution.py:669

commit v5 on v4

--- a/solution.py
+++ b/solution.py
@@ -224,11 +224,11 @@
     prod, near, mine, far, out_prod, out_near, out_mine, out_far,
     err_y, err_slab, err_z, err_full,
     sum_src, out_src, sum_own, sum_y, sum_slab, sum_z, sum_full,
-    ex, ex_near, ex_mine, ex_far, ex_part, ex_y, ex_z, left_all,
+    ex, ex_near, ex_mine, ex_far, ex_part, ex_y, ex_z, left_part, left_z, left_all,
     s_near, r_near, s_far, r_far, s_fo, r_fo,
     s_ey, r_ey, s_ez, r_ez, s_ezz, r_ezz, s_eyy, r_eyy,
     s_ty, r_ty, s_tz, r_tz, s_tzz, r_tzz, s_tyy, r_tyy,
-    s_xn, r_xn, s_xf, r_xf, s_xy, r_xy, s_xz, r_xz, s_xx, r_xx, s_xs, r_xs, s_l, r_l,
+    s_xn, r_xn, s_xf, r_xf, s_xy, r_xy, s_xz, r_xz, s_xx, r_xx, s_lz, r_lz, s_ly, r_ly,
 ):
     dp, mp = lax.axis_index("dp"), lax.axis_index("mp")
     z, y, x, core = dp // N_Y, dp % N_Y, mp // 2, mp % 2
@@ -260,7 +260,7 @@
     near_first = tuple(reversed(z_steps))
 
     barrier = pltpu.get_barrier_semaphore()
-    peers = [z_peer(s) for s in z_steps] + [y_peer(s) for s in four] + [x_peer(s) for s in four] + [sibling]
+    peers = [z_peer(s) for s in z_steps] + [y_peer(s) for s in four] + [{"mp": (mp + s) % N_MP} for s in range(1, N_MP)]
     for target in peers:
         pl.semaphore_signal(barrier, inc=1, device_id=target, device_id_type=MESH)
 
@@ -292,33 +292,39 @@
         allowed.append(square == square.T)
 
     def heads(pair):
-        at = [pl.ds(pl.multiple_of(k * WIDTH + pair * 128, 128), 128) for k in range(3)]
-        grads = [[], []]
+        at = [pl.ds(k * WIDTH + pair * 128, 128) for k in range(3)]
+        cases = [(w, t) for w in range(WIN) for t in range(2)]
+        rows = [pl.ds(w * SPAN, SPAN) for w in range(WIN)]
+        q = [proj[r, at[0]] * scale for r in rows]
+        key = [proj[r, at[1]] for r in rows]
+        value = [proj[r, at[2]] for r in rows]
+        key_scaled = [k * scale for k in key]
+        grad = [mixgrad[r, at[0]] for r in rows]
+        scores = [nt(q[w] * halves[t], key[w]) for w, t in cases]
+        prob_grad = [nt(grad[w] * halves[t], value[w]) for w, t in cases]
+        scores = [jnp.where(allowed[w], v + bias_ref[2 * pair + t], MASKED) for (w, t), v in zip(cases, scores)]
+        tops = [jnp.max(v, axis=-1, keepdims=True) for v in scores]
+        exps = [jnp.exp(v - top) for v, top in zip(scores, tops)]
+        sums = [jnp.sum(v, axis=-1, keepdims=True) for v in exps]
+        prob = [v * (1.0 / total) for v, total in zip(exps, sums)]
+        prob_b = [v.astype(BF16) for v in prob]
+        weighted = [p * g for p, g in zip(prob, prob_grad)]
+        shifts = [jnp.sum(v, axis=-1, keepdims=True) for v in weighted]
+        out = [nn(v, value[w]) for (w, t), v in zip(cases, prob_b)]
+        value_grad = [tn(v, grad[w]) for (w, t), v in zip(cases, prob_b)]
+        score_grad = [p * (g - shift) for p, g, shift in zip(prob, prob_grad, shifts)]
+        score_b = [v.astype(BF16) for v in score_grad]
+        query_grad = [nn(v, key_scaled[w]) for (w, t), v in zip(cases, score_b)]
+        key_grad = [tn(v, q[w]) for (w, t), v in zip(cases, score_b)]
         for w in range(WIN):
-            rows = pl.ds(w * SPAN, SPAN)
-            q = proj[rows, at[0]] * scale
-            key = proj[rows, at[1]]
-            value = proj[rows, at[2]]
-            key_scaled = key * scale
-            grad = mixgrad[rows, at[0]]
-            parts = []
-            for t in range(2):
-                scores = nt(q * halves[t], key) + bias_ref[2 * pair + t]
-                scores = jnp.where(allowed[w], scores, MASKED)
-                exps = jnp.exp(scores - jnp.max(scores, axis=-1, keepdims=True))
-                prob = exps * (1.0 / jnp.sum(exps, axis=-1, keepdims=True))
-                prob_b = prob.astype(BF16)
-                out = nn(prob_b, value)
-                prob_grad = nt(grad * halves[t], value)
-                value_grad = tn(prob_b, grad)
-                score_grad = prob * (prob_grad - jnp.sum(prob * prob_grad, axis=-1, keepdims=True))
-                grads[t].append(score_grad)
-                score_b = score_grad.astype(BF16)
-                parts.append((nn(score_b, key_scaled), tn(score_b, q), value_grad, out))
-            joined = [jnp.where(first_half, a, b).astype(BF16) for a, b in zip(*parts)]
+            joined = [
+                jnp.where(first_half, v[2 * w], v[2 * w + 1]).astype(BF16)
+                for v in (query_grad, key_grad, value_grad, out)
+            ]
             for k in range(3):
-                packed[rows, at[k]] = joined[k]
-            mixed[rows, :] = joined[3]
+                packed[rows[w], at[k]] = joined[k]
+            mixed[rows[w], :] = joined[3]
+        grads = [[score_grad[t], score_grad[2 + t]] for t in range(2)]
         for t in range(2):
             total = grads[t][0] + grads[t][1]
             high = total.astype(BF16).astype(F32)
@@ -326,8 +332,7 @@
             score_low[2 * pair + t] = total - high
         return at
 
-    order = (2, 1, 3, 0)
-    near_in, near_out, far_in, far_out = {}, {}, {}, {}
+    near_in, near_out, far_in = {}, {}, {}
 
     def send_near(i, at):
         columns = jnp.concatenate([packed[:, at[k]] for k in range(3)], axis=1)
@@ -345,16 +350,19 @@
         for s in four:
             chip = (x + s) % N_X
             mine[i, s] = (prod[i, chip, core].astype(F32) + near[i, chip].astype(F32)).astype(BF16)
-            pair = pair_of(i)
-            far_in[i, s] = remote(mine.at[i, s], far.at[pair, s], s_far.at[i, s], r_far.at[pair, s], x_peer(s))
+            far_in[i, s] = remote(mine.at[i, s], far.at[i, s], s_far.at[i, s], r_far.at[i, s], x_peer(s))
         near_out[i].wait_recv()
-        s = order[i]
-        if s:
-            out_mine[s] = (out_prod[i, core].astype(F32) + out_near[i].astype(F32)).astype(BF16)
-            far_out[s] = remote(out_mine.at[s], out_far.at[s], s_fo.at[s], r_fo.at[s], x_peer(s))
-
-    def pair_of(i):
-        return (x + order[i]) % N_X
+        out_mine[i] = (out_prod[i, core].astype(F32) + out_near[i].astype(F32)).astype(BF16)
+        for s in four:
+
+            @pl.when((x + s) % N_X == i)
+            def _(s=s):
+                far_out(i, s).start()
+
+    def far_out(i, s):
+        return pltpu.make_async_remote_copy(
+            out_mine.at[i], out_far.at[s], s_fo.at[s], r_fo.at[s], device_id=x_peer(s), device_id_type=MESH
+        )
 
     e_y = []
 
@@ -367,7 +375,7 @@
             )
 
     for i in range(4):
-        at = heads(pair_of(i))
+        at = heads(i)
         if i == 0:
             pl.semaphore_wait(barrier, len(peers))
         send_near(i, at)
@@ -403,6 +411,31 @@
     tokgrad_ref[...] = (cot_ref[...].astype(F32) + delta).astype(BF16)
 
     send_far(3)
+
+    t_y = {}
+
+    def send_y(j, total, src, width):
+        src[...] = total.astype(BF16)
+        for s in four:
+            rows = slab_rows((y + s) % N_Y)
+            t_y[j, s] = remote(
+                src.at[rows], sum_y.at[j, s, :, pl.ds(0, width)], s_ty.at[j, s], r_ty.at[j, s], y_peer(s)
+            )
+
+    def sum_chunk(i):
+        total = prod[i, x, core].astype(F32) + near[i, x].astype(F32)
+        for s in (1, 3, 2):
+            far_in[i, s].wait_recv()
+            total = total + far[i, s].astype(F32)
+        total = total * (1.0 / N_MP)
+        for k in range(3):
+            cols = pl.ds(k * WIDTH + i * 128, 128)
+            merged[:, cols] = total[:, 128 * k : 128 * (k + 1)] + in_error[:, cols]
+        send_y(i, total, sum_src.at[i], 384)
+        sum_own[i, :, :384] = total
+
+    for i in range(2):
+        sum_chunk(i)
 
     chunk_row = lax.broadcasted_iota(jnp.int32, (8, SPAN), 0)
     within = lax.broadcasted_iota(jnp.int32, (128, SPAN), 0)
@@ -436,37 +469,6 @@
         s: remote(ex.at[(x + s) % N_X, 1 - core], ex_near.at[s], s_xn.at[s], r_xn.at[s], sibling) for s in (2, 1, 3, 0)
     }
 
-    t_y = {}
-    totals = []
-
-    def send_y(j, total, src, width):
-        src[...] = total.astype(BF16)
-        for s in four:
-            rows = slab_rows((y + s) % N_Y)
-            t_y[j, s] = remote(
-                src.at[rows], sum_y.at[j, s, :, pl.ds(0, width)], s_ty.at[j, s], r_ty.at[j, s], y_peer(s)
-            )
-
-    for i in range(4):
-        total = prod[i, x, core].astype(F32) + near[i, x].astype(F32)
-        for s in (1, 3, 2):
-            far_in[i, s].wait_recv()
-            total = total + far[pair_of(i), s].astype(F32)
-        total = total * (1.0 / N_MP)
-        for k in range(3):
-            cols = pl.ds(pl.multiple_of(k * WIDTH + pair_of(i) * 128, 128), 128)
-            merged[:, cols] = total[:, 128 * k : 128 * (k + 1)] + in_error[:, cols]
-        send_y(i, total, sum_src.at[i], 384)
-        sum_own[i, :, :384] = total
-    total = out_prod[3, core].astype(F32) + out_near[3].astype(F32)
-    for s in (2, 1, 3):
-        far_out[s].wait_recv()
-        total = total + out_far[s].astype(F32)
-    total = total * (1.0 / N_MP)
-    merged[:, split:] = total + out_error[...]
-    send_y(4, total, out_src, WIDTH)
-    sum_own[4] = total
-
     piece = err_slab[z]
     for s in near_first:
         e_z[s].wait_recv()
@@ -475,6 +477,17 @@
     here = err_full.at[y, z]
     e_zz = {s: remote(here, here, s_ezz.at[s], r_ezz.at[s], z_peer(s)) for s in z_steps}
 
+    for i in range(2, 4):
+        sum_chunk(i)
+    total = out_prod[x, core].astype(F32) + out_near[x].astype(F32)
+    for s in (1, 3, 2):
+        far_out(0, s).wait_recv()
+        total = total + out_far[s].astype(F32)
+    total = total * (1.0 / N_MP)
+    merged[:, split:] = total + out_error[...]
+    send_y(4, total, out_src, WIDTH)
+    sum_own[4] = total
+
     x_far = {}
     for s in four:
         x_near[s].wait_recv()
@@ -487,12 +500,24 @@
             t_y[j, s].wait_recv()
             total = total + sum_y[j, s].astype(F32)
         for k in range(3 if j < 4 else 4):
-            piece_at = 4 * k + pair_of(j) if j < 4 else 12 + k
+            piece_at = 4 * k + j if j < 4 else 12 + k
             sum_slab[piece_at] = total[:, 128 * k : 128 * (k + 1)]
     rounded = sum_slab[...].astype(BF16)
     sum_send = sum_full.at[N_Y]
     sum_full[N_Y] = rounded
     t_z = {s: remote(sum_send.at[(z + s) % N_Z], sum_z.at[s], s_tz.at[s], r_tz.at[s], z_peer(s)) for s in z_steps}
+
+    def left_rows(ref, *at):
+        wide = jnp.concatenate([ref[*at, k] for k in range(N_Z)], axis=1)
+        both = jnp.concatenate(
+            [nt(wide[:, :split], in_basis[...], precision=HIGH), nt(wide[:, split:], out_basis[...], precision=HIGH)],
+            axis=1,
+        )
+        return jnp.concatenate([both[:8], both[8:]], axis=1)
+
+    left = left_rows(sum_slab) * (1.0 / (N_Y * N_Z))
+    left_part[...] = left
+    l_z = {s: remote(left_part, left_z.at[s], s_lz.at[s], r_lz.at[s], z_peer(s)) for s in z_steps}
 
     x_near[0].wait_recv()
     part = ex[x, core] + ex_near[0]
@@ -502,6 +527,18 @@
     ex_part[0] = part
     x_y = {s: remote(ex_part.at[0], ex_y.at[s], s_xy.at[s], r_xy.at[s], y_peer(s)) for s in four}
 
+    for s in near_first:
+        e_zz[s].wait_recv()
+    here = err_full.at[y]
+    e_yy = {s: remote(here, here, s_eyy.at[s], r_eyy.at[s], y_peer(s)) for s in four}
+    left = left + left_rows(err_full, y)
+
+    for s in four:
+        x_y[s].wait_recv()
+        part = part + ex_y[s]
+    ex_part[1] = part
+    x_z = {s: remote(ex_part.at[1], ex_z.at[s], s_xz.at[s], r_xz.at[s], z_peer(s)) for s in z_steps}
+
     piece = sum_slab[z]
     for s in near_first:
         t_z[s].wait_recv()
@@ -511,59 +548,51 @@
     t_zz = {s: remote(here, here, s_tzz.at[s], r_tzz.at[s], z_peer(s)) for s in z_steps}
 
     for s in near_first:
-        e_zz[s].wait_recv()
-    here = err_full.at[y]
-    e_yy = {s: remote(here, here, s_eyy.at[s], r_eyy.at[s], y_peer(s)) for s in four}
-
-    for s in four:
-        x_y[s].wait_recv()
-        part = part + ex_y[s]
-    ex_part[1] = part
-    x_z = {s: remote(ex_part.at[1], ex_z.at[s], s_xz.at[s], r_xz.at[s], z_peer(s)) for s in z_steps}
+        l_z[s].wait_recv()
+        left = left + left_z[s]
+    left_all[y] = left
+    here = left_all.at[y]
+    l_y = {s: remote(here, here, s_ly.at[s], r_ly.at[s], y_peer(s)) for s in four}
+
+    for s in (1, 3, 2):
+        l_y[s].wait_recv()
+    rows_of = []
+    for k in range(N_Y):
+        rows_of += [left_all[k, :, :BLOCK], left_all[k, :, BLOCK:]]
+    flipped_left = jnp.concatenate(rows_of, axis=0).T
 
     def finish(slab):
         for k in range(N_Z):
             mean[slab_rows(slab), 128 * k : 128 * (k + 1)] = err_full[slab, k] + sum_full[slab, k].astype(F32)
 
-    for s in near_first:
-        t_zz[s].wait_recv()
+    t_yy, x_x = {}, {}
+
+    def halfway():
+        for s in near_first:
+            t_zz[s].wait_recv()
+        here = sum_full.at[y]
+        for s in four:
+            t_yy[s] = remote(here, here, s_tyy.at[s], r_tyy.at[s], y_peer(s))
+        total = part
+        for s in near_first:
+            x_z[s].wait_recv()
+            total = total + ex_z[s]
+        extra_all[mp] = total
+        here = extra_all.at[mp]
+        for s in range(1, N_MP):
+            x_x[s] = remote(here, here, s_xx.at[s], r_xx.at[s], {"mp": (mp + s) % N_MP})
+
+    ortho[...] = orthonormal_rows(jnp.concatenate([flipped_left[:32], flipped_left[32:]], axis=1), halfway)
+
     finish(y)
-
-    slab = mean[slab_rows(y), :]
-    in_left = nt(slab[:, :split], in_basis[...], precision=HIGH)
-    out_left = nt(slab[:, split:], out_basis[...], precision=HIGH)
-    left_all[y] = jnp.concatenate([in_left, out_left, jnp.zeros((16, 64), F32)], axis=1)
-    here = left_all.at[y]
-    left_y = {s: remote(here, here, s_l.at[s], r_l.at[s], y_peer(s)) for s in four}
-    here = sum_full.at[y]
-    t_yy = {s: remote(here, here, s_tyy.at[s], r_tyy.at[s], y_peer(s)) for s in four}
-
-    for s in near_first:
-        x_z[s].wait_recv()
-        part = part + ex_z[s]
-    extra_all[mp] = part
-    here = extra_all.at[mp]
-    x_x = {s: remote(here, here, s_xx.at[s], r_xx.at[s], x_peer(s)) for s in four}
-    x_s = [remote(here, here, s_xs.at[0], r_xs.at[0], sibling)]
-
-    for s in (1, 3, 2):
-        left_y[s].wait_recv()
-    flipped_left = left_all[...].reshape(BLOCK, 128).T
-
-    def halfway():
-        for s in (1, 3, 2):
-            x_x[s].wait_recv()
-            here = extra_all.at[2 * ((x + N_X - s) % N_X) + core]
-            x_s.append(remote(here, here, s_xs.at[s], r_xs.at[s], sibling))
-
-    ortho[...] = orthonormal_rows(jnp.concatenate([flipped_left[:32], flipped_left[32:64]], axis=1), halfway)
-
     for s in (1, 3, 2):
         e_yy[s].wait_recv()
         t_yy[s].wait_recv()
         finish((y + N_Y - s) % N_Y)
-    for copy in x_s:
+    for copy in x_x.values():
         copy.wait_recv()
+    for s in four:
+        far_out(0, s).wait_send()
     for copy in sent:
         copy.wait_send()
 
@@ -622,12 +651,14 @@
             vmem(2, 8, 128),
             vmem(N_Y, 8, 128),
             vmem(N_Z, 8, 128),
-            vmem(N_Y, 16, 128),
+            vmem(8, 128),
+            vmem(N_Z, 8, 128),
+            vmem(N_Y, 8, 128),
         ]
         + dma(4, 2) + dma(4, 4) + dma(4)
         + dma(4, 2) + dma(N_Z) + dma(N_Z) + dma(4)
         + dma(5, 4) + dma(N_Z) + dma(N_Z) + dma(4)
-        + dma(4) + dma(4) + dma(4) + dma(N_Z) + dma(4) + dma(4) + dma(4),
+        + dma(4) + dma(4) + dma(4) + dma(N_Z) + dma(N_MP) + dma(N_Z) + dma(4),
         compiler_params=pltpu.CompilerParams(collective_id=1, has_side_effects=True, vmem_limit_bytes=48 << 20),
         name="layer",
     )(*(pltpu.with_memory_space_constraint(a, pltpu.HBM) for a in operands[:9]), *operands[9:])

time: 85.1 us -> 82.4 us (0.968)
  Pallas kernels: 84.2 us -> 81.6 us
    pallas_call x1, Pallas kernels: 63.3 us -> 60.7 us  [layer(): pl.pallas_call(layer_kernel, out_shape=(jax.ShapeDtypeStruct((ROWS, WIDTH...]
where the time goes in v5:
time: 82.4 us; the launch traced here: 82.2 us
  Pallas kernels  81.6 us (99%)
    pallas_call x1, Pallas kernels, layer(): pl.pallas_call(layer_kernel, out_shape=(jax.ShapeDtypeStruct((ROWS, WIDTH...  60.7 us
    pallas_call x1, Pallas kernels, gather_weights(): pl.pallas_call(gather_kernel, out_shape=(jax.ShapeDtypeStruct((WIDTH, 3 *...  19 us
    pallas_call x1, Pallas kernels, factors(): pl.pallas_call(factor_kernel, out_shape=(wide, thin, wide, thin, jax.Shap...  1.84 us

profile of v5, /device:TPU:1, one launch (start us, length us, event | category | flops | bytes accessed | tf_op | source)
XLA Modules:
  0.0 82.2 jit_solution(12947786253345363454)
XLA Ops:
  0.6 19.0 %gather_weights.1 = (bf16[512,1536]{1,0:T(8,128)(2,1)S(1)}, bf16[512,512]{1,0:T(8,128)(2,1)S(1)}, f32[8,144,144]{2,1,0:T(8,128)S(1)}, bf16[288,512]{1,0:T(8,128)(2,1)S(1)}, bf16[512,288]{1,0:T(8,128)(2,1)S(1)}) custom-call(bf16[64,1536]{1,0:T(8,128)(2,1)} %in_ref.1, bf16[64,512]{1,0:T(8,128)(2,1)} %out_ref.1, f32[8,759]{1,0:T(8,128)} %table_hbm.1, ...), custom_call_target="tpu_custom_call" | custom-call | tf_op jit(solution)/shard_map/gather_weights/pallas_call | solution.py:158
  19.7 60.7 %layer.1 = (bf16[288,512]{1,0:T(8,128)(2,1)S(1)}, f32[64,2048]{1,0:T(8,128)S(1)}, f32[64,2048]{1,0:T(8,128)S(1)}, f32[8,8,128]{2,1,0:T(8,128)S(1)}, f32[32,128]{1,0:T(8,128)S(1)}) custom-call(bf16[288,512]{1,0:T(8,128)(2,1)} %bitcast.24, s32[2,144]{1,0:T(2,128)} %region_hbm.1, f32[64,1536]{1,0:T(8,128)} %bitcast.23, f32[64,512]{1,0:T(8,128)} %bitcast.26, ...), custom_call_target="tpu_custom_call" | custom-call | tf_op jit(solution)/shard_map/layer/pallas_call | solution.py:607
  80.4 1.8 %factors.1 = (f32[64,1536]{1,0:T(8,128)}, f32[64,512]{1,0:T(8,128)}, f32[64,1536]{1,0:T(8,128)}, f32[64,512]{1,0:T(8,128)}, f32[32,1536]{1,0:T(8,128)}, /*index=...) custom-call(f32[64,2048]{1,0:T(8,128)S(1)} %get-tuple-element.33.mean, ...), custom_call_target="tpu_custom_call" | custom-call | tf_op jit(solution)/shard_map/factors/pallas_call | solution.py:700

commit v6 on v5

--- a/solution.py
+++ b/solution.py
@@ -191,7 +191,7 @@
     in_w, out_w, in_wr, out_wr, squares = ([zero] * 4 for _ in range(5))
     for c in range(32):
         g, at = c // 8, c % 8
-        if c == 16:
+        if c == 8:
             halfway()
         here = row == at
         vector = jnp.broadcast_to((columns[g] - taken[g])[at : at + 1, :], (8, 128))
@@ -374,13 +374,11 @@
                 remote(out_error.at[rows], err_y.at[s, :, pl.ds(split, WIDTH)], s_ey.at[s, 1], r_ey.at[s, 1], y_peer(s))
             )
 
+    pl.semaphore_wait(barrier, len(peers))
+    error_over_y()
     for i in range(4):
         at = heads(i)
-        if i == 0:
-            pl.semaphore_wait(barrier, len(peers))
         send_near(i, at)
-        if i == 0:
-            error_over_y()
         if i:
             send_far(i - 1)
 
@@ -507,15 +505,12 @@
     sum_full[N_Y] = rounded
     t_z = {s: remote(sum_send.at[(z + s) % N_Z], sum_z.at[s], s_tz.at[s], r_tz.at[s], z_peer(s)) for s in z_steps}
 
-    def left_rows(ref, *at):
-        wide = jnp.concatenate([ref[*at, k] for k in range(N_Z)], axis=1)
-        both = jnp.concatenate(
-            [nt(wide[:, :split], in_basis[...], precision=HIGH), nt(wide[:, split:], out_basis[...], precision=HIGH)],
-            axis=1,
-        )
-        return jnp.concatenate([both[:8], both[8:]], axis=1)
-
-    left = left_rows(sum_slab) * (1.0 / (N_Y * N_Z))
+    wide = jnp.concatenate([sum_slab[k] + err_slab[k] for k in range(N_Z)], axis=1)
+    both = jnp.concatenate(
+        [nt(wide[:, :split], in_basis[...], precision=HIGH), nt(wide[:, split:], out_basis[...], precision=HIGH)],
+        axis=1,
+    )
+    left = jnp.concatenate([both[:8], both[8:]], axis=1) * (1.0 / (N_Y * N_Z))
     left_part[...] = left
     l_z = {s: remote(left_part, left_z.at[s], s_lz.at[s], r_lz.at[s], z_peer(s)) for s in z_steps}
 
@@ -531,7 +526,6 @@
         e_zz[s].wait_recv()
     here = err_full.at[y]
     e_yy = {s: remote(here, here, s_eyy.at[s], r_eyy.at[s], y_peer(s)) for s in four}
-    left = left + left_rows(err_full, y)
 
     for s in four:
         x_y[s].wait_recv()

time: 82.4 us -> 80.4 us (0.976)
  Pallas kernels: 81.6 us -> 79.4 us
    pallas_call x1, Pallas kernels: 60.7 us -> 58.5 us  [layer(): pl.pallas_call(layer_kernel, out_shape=(jax.ShapeDtypeStruct((ROWS, WIDTH...]
where the time goes in v6:
time: 80.4 us; the launch traced here: 80 us
  Pallas kernels  79.4 us (99%)
    pallas_call x1, Pallas kernels, layer(): pl.pallas_call(layer_kernel, out_shape=(jax.ShapeDtypeStruct((ROWS, WIDTH...  58.5 us
    pallas_call x1, Pallas kernels, gather_weights(): pl.pallas_call(gather_kernel, out_shape=(jax.ShapeDtypeStruct((WIDTH, 3 *...  19 us
    pallas_call x1, Pallas kernels, factors(): pl.pallas_call(factor_kernel, out_shape=(wide, thin, wide, thin, jax.Shap...  1.83 us

profile of v6, /device:TPU:1, one launch (start us, length us, event | category | flops | bytes accessed | tf_op | source)
XLA Modules:
  0.0 80.0 jit_solution(3271359550972711845)
XLA Ops:
  0.6 19.0 %gather_weights.1 = (bf16[512,1536]{1,0:T(8,128)(2,1)S(1)}, bf16[512,512]{1,0:T(8,128)(2,1)S(1)}, f32[8,144,144]{2,1,0:T(8,128)S(1)}, bf16[288,512]{1,0:T(8,128)(2,1)S(1)}, bf16[512,288]{1,0:T(8,128)(2,1)S(1)}) custom-call(bf16[64,1536]{1,0:T(8,128)(2,1)} %in_ref.1, bf16[64,512]{1,0:T(8,128)(2,1)} %out_ref.1, f32[8,759]{1,0:T(8,128)} %table_hbm.1, ...), custom_call_target="tpu_custom_call" | custom-call | tf_op jit(solution)/shard_map/gather_weights/pallas_call | solution.py:158
  19.7 58.5 %layer.1 = (bf16[288,512]{1,0:T(8,128)(2,1)S(1)}, f32[64,2048]{1,0:T(8,128)S(1)}, f32[64,2048]{1,0:T(8,128)S(1)}, f32[8,8,128]{2,1,0:T(8,128)S(1)}, f32[32,128]{1,0:T(8,128)S(1)}) custom-call(bf16[288,512]{1,0:T(8,128)(2,1)} %bitcast.24, s32[2,144]{1,0:T(2,128)} %region_hbm.1, f32[64,1536]{1,0:T(8,128)} %bitcast.23, f32[64,512]{1,0:T(8,128)} %bitcast.26, ...), custom_call_target="tpu_custom_call" | custom-call | tf_op jit(solution)/shard_map/layer/pallas_call | solution.py:601
  78.2 1.8 %factors.1 = (f32[64,1536]{1,0:T(8,128)}, f32[64,512]{1,0:T(8,128)}, f32[64,1536]{1,0:T(8,128)}, f32[64,512]{1,0:T(8,128)}, f32[32,1536]{1,0:T(8,128)}, /*index=...) custom-call(f32[64,2048]{1,0:T(8,128)S(1)} %get-tuple-element.33.mean, ...), custom_call_target="tpu_custom_call" | custom-call | tf_op jit(solution)/shard_map/factors/pallas_call | solution.py:694
